TPU v7x, 256 devices: a whole 4x4x8 slice. The times are simulated.
256 devices in a mesh: dp: 64 (over x, z, core), chan: 4 (over y).
Axes of the slice: x: 4, y: 4, z: 8, core: 2. Of those that a mesh axis runs over, the one named last changes fastest.
Arguments:
- activations: bfloat16 [640, 262144], P('chan', 'dp'), may hold values from -6 to 6
- out_grad: bfloat16 [640, 262144], P('chan', 'dp'), may hold values from -6 to 6
- kernel: bfloat16 [640, 5760], P('chan'), may hold values from -0.078125 to 0.078125
- error_in: float32 [64, 640, 5760], P('dp', 'chan'), may hold values from -6 to 6
- q_prev: float32 [640, 4], P('chan'), may hold values from -6 to 6
Outputs:
- in_grad: bfloat16 [640, 262144], P('chan', 'dp')
- q_factor: float32 [640, 4], P('chan')
- new_error: float32 [64, 640, 5760], P('dp', 'chan')
All inputs are finite; a program needn't handle non-finite values.
Results may differ from a plain program's by a relative error of at most 0.001.
Values may be sent and summed in bfloat16 or wider, within the bound.
No kernel may reach another device: no remote copies, remote signals or barrier semaphores. Data moves between devices by JAX's collectives and lax.ppermute only.
A program may use at most 128 MiB of HBM per device.

v0:
```python
import functools

import jax
import jax.numpy as jnp
from jax import lax
from jax.experimental import pallas as pl
from jax.experimental.pallas import tpu as pltpu
from jax.sharding import PartitionSpec as P

LAT = 64
CELLS = LAT * LAT
TAPS = 9
F32 = jnp.float32
BF16 = jnp.bfloat16
NT = (((1,), (1,)), ((), ()))
NN = (((1,), (0,)), ((), ()))
HI = lax.Precision.HIGHEST
ROLLED = BF16


def tap(t):
    return t // 3 - 1, t % 3 - 1


def dot(a, b, dims):
    return lax.dot_general(a, b, dims, preferred_element_type=F32)


def split3(v):
    hi = v.astype(BF16).astype(F32)
    rest = v - hi
    mid = rest.astype(BF16).astype(F32)
    return jnp.concatenate([hi, mid, rest - mid], axis=0).astype(BF16)


def lanes(shape):
    return lax.broadcasted_iota(jnp.int32, shape, 1)


def moved(v, t, sign=1):
    da, db = (sign * d for d in tap(t))
    off = da * LAT + db
    if off == 0:
        return v
    cell = lanes(v.shape)
    row, col = cell >> 6, cell & 63
    ok = None
    if da == 1:
        ok = row >= 1
    elif da == -1:
        ok = row < LAT - 1
    if db:
        inside = col >= 1 if db == 1 else col < LAT - 1
        ok = inside if ok is None else ok & inside
    return jnp.where(ok, pltpu.roll(v, off % CELLS, 1), 0.0)


def upper(v):
    return lax.broadcasted_iota(jnp.int32, v.shape, 0) % 8 < 4


def fold(v8):
    half = CELLS // 2
    return jnp.where(upper(v8[:, :half]), v8[:, :half], v8[:, half:])


def unfold(f):
    other = pltpu.roll(f, 4, 0)
    up = upper(f)
    return jnp.concatenate([jnp.where(up, f, other), jnp.where(up, other, f)], axis=1)


FOLD = CELLS // 2
GROUPS = 5
PAY = FOLD + GROUPS * 256


def ungroup(ref, start, ch):
    return jnp.concatenate([ref[:, start + 256 * i : start + 256 * i + ch] for i in range(GROUPS)], axis=0)


def start_kernel(j_ref, qt_ref, g_ref, e_ref, o0, o1, o2, o3, qb, rows, blocks, wide):
    ch = g_ref.shape[0]
    j = j_ref[0]
    wide[...] = jnp.zeros_like(wide)
    wide[0:4, :ch] = qt_ref[...]
    wide[4:8, :ch] = qt_ref[...]
    y3 = dot(split3(wide[0:8, :ch]), g_ref[...], NN)
    y8 = y3[0:8] + y3[8:16] + y3[16:24]
    y = fold(y8)
    q = jnp.transpose(wide[...])[:ch, :]
    for r in range(4):
        qb[r] = jnp.broadcast_to(q[:, r : r + 1], (ch, 128))
    rows[...] = jnp.zeros_like(rows)
    for t in range(TAPS):
        for v in range(5):
            at = t * 640 + v * 128
            acc = [jnp.zeros((8, 128), F32) for _ in range(4)]
            for c in range(0, ch, 8):
                e = e_ref[c : c + 8, at : at + 128]
                for r in range(4):
                    acc[r] = acc[r] + e * qb[r, c : c + 8, :]
            for r in range(4):
                rows[t * 4 + r : t * 4 + r + 1, v * 128 : (v + 1) * 128] = jnp.sum(acc[r], axis=0, keepdims=True)
    for k in range(4):
        r640 = rows[...]
        if k:
            r640 = pltpu.roll(r640, 640 - k * ch, 1)
        for i in range(GROUPS):
            blocks[k, :, 256 * i : 256 * (i + 1)] = r640[8 * i : 8 * i + 8, :256]
    for s, out in enumerate((o0, o1, o2, o3)):
        out[:, :FOLD] = y
        out[:, FOLD:] = blocks[lax.rem(j + s, 4)]


def sketch_kernel(own, r1, r2, r3, x_ref, out, stack, rows):
    ch = x_ref.shape[0]
    total = own[...] + r1[...] + r2[...] + r3[...]
    y8 = unfold(total[:, :FOLD])
    up = upper(y8)
    for i in range(GROUPS):
        second = moved(y8, 2 * i + 1) if 2 * i + 1 < TAPS else jnp.zeros_like(y8)
        stack[8 * i : 8 * i + 8, :] = jnp.where(up, moved(y8, 2 * i), second)
    c3 = dot(split3(stack[...]), x_ref[...], NT)
    c = (c3[0:40] + c3[40:80] + c3[80:120]) * (1.0 / LAT)
    rows[...] = jnp.zeros_like(rows)
    for i in range(GROUPS):
        at = 256 * i
        rows[:, at : at + ch] = c[8 * i : 8 * i + 8] + total[:, FOLD + at : FOLD + at + ch]
    for k in range(out.shape[0]):
        out[k] = rows[...]


def total_kernel(got, out):
    total = got[0]
    for k in range(1, got.shape[0]):
        total = total + got[k]
    for k in range(out.shape[0]):
        out[k] = total


def image_kernel(scale, s_ref, x_ref, out, taps):
    ch = x_ref.shape[0]
    sk = s_ref[0]
    for k in range(1, s_ref.shape[0]):
        sk = sk + s_ref[k]
    sk = sk * scale
    m = jnp.concatenate([sk[:, 256 * i : 256 * i + ch] for i in range(GROUPS)], axis=0)
    u3 = dot(split3(m), x_ref[...], NN)
    taps[...] = u3[0:40] + u3[40:80] + u3[80:120]
    z8 = jnp.zeros((8, CELLS), F32)
    up = upper(z8)
    for i in range(GROUPS):
        u = taps[8 * i : 8 * i + 8, :]
        second = moved(u, 2 * i + 1, -1) if 2 * i + 1 < TAPS else jnp.zeros_like(u)
        z8 = z8 + jnp.where(up, moved(u, 2 * i, -1), second)
    z8 = z8 + pltpu.roll(z8, 4, 0)
    folded = fold(z8)
    for k in range(4):
        out[k, :, :FOLD] = folded
        out[k, :, FOLD:] = sk


def forward_substitution(low, rows):
    done = []
    for r in range(4):
        v = rows[r]
        for s in range(r):
            v = v - low[r][s] * done[s]
        done.append(v / low[r][r])
    return done


def factor_kernel(blocks, e_ref, g_ref, basis_ref, q_out, by_rank, acc_ref):
    ch = g_ref.shape[0]
    z8 = unfold(blocks[0, :, :FOLD] + blocks[1, :, :FOLD] + blocks[2, :, :FOLD] + blocks[3, :, :FOLD])
    wide = jnp.zeros((40, 640), F32)
    lane = lanes((40, 640))
    for k in range(4):
        b = jnp.concatenate([blocks[k, :, FOLD + 256 * i : FOLD + 256 * (i + 1)] for i in range(GROUPS)], axis=0)
        b = jnp.concatenate([b, jnp.zeros((40, 384), F32)], axis=1)
        if k:
            b = pltpu.roll(b, k * ch, 1)
        wide = jnp.where((lane >= k * ch) & (lane < (k + 1) * ch), b, wide)
    by_rank[...] = jnp.zeros_like(by_rank)
    for t in range(TAPS):
        for r in range(4):
            by_rank[r, t : t + 1, :] = wide[t * 4 + r : t * 4 + r + 1]
    rows = [by_rank[r] for r in range(4)]
    low = [[None] * 4 for _ in range(4)]
    for r in range(4):
        for s in range(r + 1):
            v = jnp.sum(rows[r] * rows[s], keepdims=True)
            for k in range(s):
                v = v - low[r][k] * low[s][k]
            low[r][s] = jnp.sqrt(v) if r == s else v / low[s][s]
    basis = forward_substitution(low, rows)
    for r in range(4):
        basis_ref[r * 16 : (r + 1) * 16, :] = basis[r]
    z = forward_substitution(low, [z8[r : r + 1] for r in range(4)])
    z = jnp.concatenate(z + [jnp.zeros((4, CELLS), F32)], axis=0)
    q3 = dot(split3(z), g_ref[...], NT)
    q = (q3[0:8] + q3[8:16] + q3[16:24]) * (1.0 / LAT)
    for c0 in range(0, ch, 32):
        acc = [[jnp.zeros((8, 128), F32) for _ in range(4)] for _ in range(4)]
        for t in range(TAPS):
            for v in range(5):
                at = t * 640 + v * 128
                es = [e_ref[c0 + 8 * i : c0 + 8 * i + 8, at : at + 128] for i in range(4)]
                for r in range(4):
                    b = jnp.broadcast_to(basis_ref[r * 16 + t : r * 16 + t + 1, v * 128 : (v + 1) * 128], (8, 128))
                    for i in range(4):
                        acc[i][r] = acc[i][r] + es[i] * b
        for i in range(4):
            for r in range(4):
                acc_ref[r, c0 + 8 * i : c0 + 8 * i + 8, :] = acc[i][r]
    ones = jnp.ones((8, 128), F32)
    row = lax.broadcasted_iota(jnp.int32, q.shape, 0)
    for r in range(4):
        part = lax.dot_general(ones, acc_ref[r], NT, precision=HI, preferred_element_type=F32)
        q = jnp.where(row == r, q + part, q)
    q = jnp.concatenate([q, jnp.zeros((8, 256 - ch), F32)], axis=1)
    q = jnp.where(upper(q[:, :128]), q[:, :128], pltpu.roll(q[:, 128:], 4, 0))
    for k in range(q_out.shape[0]):
        q_out[k] = q


def right_factor(got, wide, ch):
    total = got[0]
    for k in range(1, got.shape[0]):
        total = total + got[k]
    wide[...] = jnp.zeros_like(wide)
    wide[:8, :128] = total
    wide[:8, 128:] = pltpu.roll(total, 4, 0)
    return jnp.transpose(wide[...])[:ch, :4] * (1.0 / got.shape[0])


def cols_moved(v, db):
    if db == 0:
        return v
    col = lanes(v.shape) & 63
    return jnp.where(col >= 1 if db == 1 else col < LAT - 1, pltpu.roll(v, db % CELLS, 1), jnp.zeros((), v.dtype))


def rows_moved(v):
    w = pltpu.roll(v, LAT, 1)
    edge = lanes((v.shape[0], 128))
    none = jnp.zeros((), v.dtype)
    down = jnp.concatenate([jnp.where(edge < LAT, none, w[:, :128]), w[:, 128:]], axis=1)
    up = jnp.concatenate([w[:, 128:], jnp.where(edge < LAT, w[:, :128], none)], axis=1)
    return up, v, down


def weight_kernel(j_ref, x0, xlt, xlb, xrt, xrb, xa, xb, g_ref, e_ref, got, basis_ref, out, q_out, stack, xs, acc, wide):
    ch = g_ref.shape[0]
    half = ch // 2
    j = j_ref[0]
    for ref, s, first in ((x0, 0, 0), (xlt, 1, 0), (xlb, 1, half), (xrt, 3, 0), (xrb, 3, half), (xa, 2, 0), (xb, 2, half)):
        at = pl.multiple_of(lax.rem(j + 4 - s, 4) * ch + first, 16)
        xs[pl.ds(at, ref.shape[0]), :] = ref[...]

    def shifted(i, carry):
        at = pl.multiple_of(i * 16, 16)
        g = g_ref[pl.ds(at, 16), :].astype(F32)
        for b in range(3):
            for a, v in enumerate(rows_moved(cols_moved(g, b - 1).astype(ROLLED))):
                stack[pl.ds((3 * a + b) * ch + at, 16), :] = v.astype(BF16)
        return carry

    lax.fori_loop(0, ch // 16, shifted, 0)
    step = 2048
    acc[...] = dot(stack[:, :step], xs[:, :step], NT)

    def more(i, carry):
        cells = pl.ds(pl.multiple_of(i * step, step), step)
        acc[...] += dot(stack[:, cells], xs[:, cells], NT)
        return carry

    lax.fori_loop(1, CELLS // step, more, 0)
    q_out[...] = right_factor(got, wide, ch)
    for t in range(TAPS):
        for c in range(0, ch, 32):
            rows, cols = slice(c, c + 32), slice(t * 640, (t + 1) * 640)
            v = acc[t * ch + c : t * ch + c + 32, :] * (1.0 / LAT) + e_ref[rows, cols]
            for r in range(4):
                v = v - q_out[rows, r : r + 1] * basis_ref[r * 16 + t : r * 16 + t + 1, :]
            out[rows, cols] = v


SIDE = 512
PIECE = SIDE // 2


def block_kernel(at_ref, k_ref, own, p1, p2, p3, wide, blocks):
    ch = k_ref.shape[0]
    j, piece = at_ref[0], at_ref[1]
    wide[...] = jnp.zeros_like(wide)
    lane = lanes((ch, 256))
    for k in range(4):
        for a in range(3):
            for b in range(3):
                base, off = divmod(k * ch, 128)
                at = (3 * a + b) * 4 * ch + base * 128
                v = k_ref[:, at : at + 256].astype(F32)
                base, goal = divmod(b * ch, 128)
                if goal != off:
                    v = pltpu.roll(v, (goal - off) % 256, 1)
                rows, cols = slice(a * ch, (a + 1) * ch), slice(base * 128, base * 128 + 256)
                wide[rows, cols] = jnp.where((lane >= goal) & (lane < goal + ch), v, wide[rows, cols])
        blocks[k] = jnp.transpose(wide[...]).astype(BF16)
    own[...] = blocks[j]
    rows = pl.ds(pl.multiple_of(piece * PIECE, PIECE), PIECE)
    for s, out in ((1, p1), (2, p2), (3, p3)):
        out[...] = blocks[lax.rem(j + s, 4), rows, :]


def rows_stacked(refs, g3, slot):
    ch = sum(ref.shape[0] for ref in refs)
    g3[slot, 3 * ch :, :] = jnp.zeros((SIDE - 3 * ch, CELLS), BF16)
    start = 0
    for ref in refs:

        def body(i, carry, ref=ref, start=start):
            at = pl.multiple_of(i * 16, 16)
            for a, v in enumerate(rows_moved(ref[pl.ds(at, 16), :].astype(ROLLED))):
                g3[slot, pl.ds(a * ch + start + at, 16), :] = v.astype(BF16)
            return carry

        lax.fori_loop(0, ref.shape[0] // 16, body, 0)
        start += ref.shape[0]


def products(blocks, g3, v_ref):
    step = 512
    used = v_ref.shape[0]

    def body(i, carry):
        cells = pl.ds(pl.multiple_of(i * step, step), step)
        total = None
        for slot, block in enumerate(blocks):
            p = dot(block[:used, :], g3[slot, :, cells], NN)
            total = p if total is None else total + p
        v_ref[:, cells] = total
        return carry

    lax.fori_loop(0, CELLS // step, body, 0)


def collected(v_ref, at, n):
    ch = v_ref.shape[0] // 3
    v = [v_ref[pl.ds(b * ch + at, n), :] for b in range(3)]
    return v[1] + cols_moved(v[0], -1) + cols_moved(v[2], 1)


def own_kernel(k_ref, g, out, g3, v_ref):
    rows_stacked((g,), g3, 0)
    products((k_ref,), g3, v_ref)

    def body(i, carry):
        at = pl.multiple_of(i * 16, 16)
        out[pl.ds(at, 16), :] = collected(v_ref, at, 16)
        return carry

    lax.fori_loop(0, out.shape[0] // 16, body, 0)


def rest_kernel(at_ref, mine_ref, other_ref, glt, glb, grt, grb, ga, go, acc_ref, out, blocks, g3, v_ref):
    first = pl.multiple_of(at_ref[1] * PIECE, PIECE)
    second = pl.multiple_of((1 - at_ref[1]) * PIECE, PIECE)
    for s, refs in enumerate(((glt, glb), (ga, go), (grt, grb))):
        blocks[s, pl.ds(first, PIECE), :] = mine_ref[s]
        blocks[s, pl.ds(second, PIECE), :] = other_ref[s]
        rows_stacked(refs, g3, s)
    products([blocks.at[s] for s in range(3)], g3, v_ref)

    def body(i, carry):
        at = pl.multiple_of(i * 16, 16)
        rows = pl.ds(at, 16)
        out[rows, :] = (collected(v_ref, at, 16) + acc_ref[rows, :]).astype(BF16)
        return carry

    lax.fori_loop(0, out.shape[0] // 16, body, 0)


def cut_kernel(v_ref, top, bottom):
    half = top.shape[0]
    top[...] = v_ref[:half, :]
    bottom[...] = v_ref[half:, :]


def call(kernel, out_shape, scratch=(), scalars=0, inputs=0, limit=60, **kw):
    whole = pl.BlockSpec(memory_space=pltpu.VMEM)
    scalar = pl.BlockSpec(memory_space=pltpu.SMEM)
    return pl.pallas_call(
        kernel,
        out_shape=out_shape,
        in_specs=[scalar] * scalars + [whole] * inputs,
        out_specs=jax.tree.map(lambda _: whole, out_shape),
        scratch_shapes=list(scratch),
        compiler_params=pltpu.CompilerParams(vmem_limit_bytes=limit << 20),
        **kw,
    )


def around(array, s):
    return lax.ppermute(array, "chan", [(i, (i + s) % 4) for i in range(4)])


def cut(block):
    half = jax.ShapeDtypeStruct((block.shape[0] // 2, block.shape[1]), block.dtype)
    return call(cut_kernel, [half, half], (), 0, 1, 8)(block)


def after(value, *others):
    return lax.optimization_barrier((value, *others))[0]


def line_groups(axis):
    if axis == "z":
        return [[x * 16 + z * 2 + c for z in range(8)] for x in range(4) for c in range(2)]
    return [[x * 16 + z * 2 + c for x in range(4) for c in range(2)] for z in range(8)]


def exchanged(array, axis):
    return lax.all_to_all(array, "dp", 0, 0, axis_index_groups=line_groups(axis), tiled=True)


def per_device(x, g, kernel, error_in, q_prev):
    ch = x.shape[0]
    workers = lax.axis_size("dp")
    j = lax.axis_index("chan").astype(jnp.int32)
    worker = lax.axis_index("dp").astype(jnp.int32)
    at = jnp.stack([j, worker % 2])
    err = error_in[0]
    sds = jax.ShapeDtypeStruct

    gt, gb = cut(g)
    glt, grb = around(gt, 1), around(gb, 3)

    pay = sds((8, PAY), F32)
    sent = call(
        start_kernel,
        [pay] * 4,
        [
            pltpu.VMEM((4, ch, 128), F32),
            pltpu.VMEM((40, 640), F32),
            pltpu.VMEM((4, 8, GROUPS * 256), F32),
            pltpu.VMEM((128, 256), F32),
        ],
        1,
        3,
        16,
    )(at, q_prev.T, g, err)
    got = [around(sent[s], s) for s in (1, 2, 3)]

    k_own, *k_sent = call(
        block_kernel,
        [sds((SIDE, SIDE), BF16)] + [sds((PIECE, SIDE), BF16)] * 3,
        [pltpu.VMEM((SIDE, SIDE), F32), pltpu.VMEM((4, SIDE, SIDE), BF16)],
        1,
        1,
        16,
    )(at, after(kernel, *sent))
    acc = call(
        own_kernel, sds((ch, CELLS), F32), [pltpu.VMEM((1, SIDE, CELLS), BF16), pltpu.VMEM((3 * ch, CELLS), F32)], 0, 2, 24
    )(k_own, g)
    got[0] = after(got[0], glt, grb, acc)

    group = sds((8, 8, GROUPS * 256), F32)
    part = call(
        sketch_kernel, group, [pltpu.VMEM((40, CELLS), F32), pltpu.VMEM((8, GROUPS * 256), F32)], 0, 5, 16
    )(sent[0], *got, x)
    part, gb, gt = lax.optimization_barrier((part, gb, gt))
    glb, grt = around(gb, 1), around(gt, 3)
    part = exchanged(part, "xc")
    part = call(total_kernel, group, (), 0, 1, 8)(part)
    glt, grb, part = lax.optimization_barrier((glt, grb, part))
    ga, go = around(glt, 1), around(grb, 3)
    part = after(exchanged(part, "z"), glb, grt)
    mine = call(
        functools.partial(image_kernel, 1.0 / workers), sds((4, 8, PAY), F32), [pltpu.VMEM((40, CELLS), F32)], 0, 2, 16
    )(part, x)
    xt, xb = cut(x)
    mine = after(mine, ga, go, xt, xb)
    theirs = lax.all_to_all(mine, "chan", 0, 0, tiled=True)
    xt, xb, theirs, *k_sent = lax.optimization_barrier((xt, xb, theirs, *k_sent))
    xlt, xrb = around(xt, 1), around(xb, 3)
    xlb, xrt = around(xb, 1), around(xt, 3)
    k_got = [around(v, s) for s, v in zip((1, 2, 3), k_sent, strict=True)]
    basis, q_part = call(
        factor_kernel,
        [sds((64, 640), F32), sds((workers, 8, 128), F32)],
        [pltpu.VMEM((4, 16, 640), F32), pltpu.VMEM((4, ch, 128), F32)],
        0,
        3,
        16,
    )(theirs, err, g)
    q_got = lax.all_to_all(q_part, "dp", 0, 0, tiled=True)
    xlt, xrb, q_got, *k_got = lax.optimization_barrier((xlt, xrb, q_got, *k_got))
    k_mine = jnp.stack(k_got)
    k_other = lax.ppermute(k_mine, "dp", [(i, i ^ 1) for i in range(workers)])
    xa, xo = around(xlt, 1), around(xrb, 3)

    in_grad = call(
        rest_kernel,
        sds((ch, CELLS), BF16),
        [pltpu.VMEM((3, SIDE, SIDE), BF16), pltpu.VMEM((3, SIDE, CELLS), BF16), pltpu.VMEM((3 * ch, CELLS), F32)],
        1,
        9,
        44,
    )(after(at, q_got), k_mine, k_other, glt, glb, grt, grb, ga, go, acc)

    new_error, q_factor = call(
        weight_kernel,
        [sds((ch, TAPS * 640), F32), sds((ch, 4), F32)],
        [
            pltpu.VMEM((TAPS * ch, CELLS), BF16),
            pltpu.VMEM((4 * ch, CELLS), BF16),
            pltpu.VMEM((TAPS * ch, 640), F32),
            pltpu.VMEM((128, 256), F32),
        ],
        1,
        11,
        44,
    )(at, x, xlt, xlb, xrt, xrb, xa, xo, g, err, after(q_got, in_grad), basis)
    return in_grad, q_factor, new_error[None]


def solution(mesh):
    in_specs = (
        P("chan", "dp"),
        P("chan", "dp"),
        P("chan", None),
        P("dp", "chan", None),
        P("chan", None),
    )
    out_specs = (P("chan", "dp"), P("chan", None), P("dp", "chan", None))
    return jax.shard_map(
        per_device, mesh=mesh, in_specs=in_specs, out_specs=out_specs, check_vma=False
    )
```

profile of v0, /device:TPU:1, one launch (start us, length us, event | category | flops | bytes accessed | tf_op | source)
XLA Modules:
  0.0 169.1 jit_solution(5012144178256018676)
XLA Ops:
  0.6 1.3 copy-done.2
  3.1 2.1 %collective-permute-start = (bf16[80,4096]{1,0:T(8,128)(2,1)}, bf16[80,4096]{1,0:T(8,128)(2,1)S(1)}, u32[]{:S(2)}, u32[]{:S(2)}) collective-permute-start(bf16[80,4096]{1,0:T(8,128)(2,1)} %get-tuple-element.57), channel_id=1, source_target_pairs={{0,1},{1,2},{2,3},{3,0},{4,5},{5,6},{6,7},{7,4},{8,9},{9,10},{10,1... | collective-permute-start | bytes 1966088 | tf_op jit(solution)/shard_map/ppermute | solution.py:406
  5.2 1.4 collective-permute-start.1
  6.7 2.0 %copy-done = f32[1,160,5760]{2,1,0:T(8,128)S(1)} copy-done((f32[1,160,5760]{2,1,0:T(8,128)S(1)}, f32[1,160,5760]{2,1,0:T(8,128)}, u32[]{:S(2)}) %copy-start) | copy-done | bytes 3686424
  9.5 2.2 %shard_map.78 = (f32[8,3328]{1,0:T(8,128)S(1)}, f32[8,3328]{1,0:T(8,128)S(1)}, f32[8,3328]{1,0:T(8,128)S(1)}, f32[8,3328]{1,0:T(8,128)S(1)}) custom-call(s32[2]{0:T(128)S(1)} %pad_add_fusion.j_ref.at_ref, f32[4,160]{1,0:T(4,128)S(1)} %bitcast.11, bf16[160,4096]{1,0:T(8,128)(2,1)S(1)} %copy-done.3, f32[160,5760]{1,0:T(8,128)S(1)} %bitcast.9), custom_call_target="tpu_custom_call" | custom-call | tf_op jit(solution)/shard_map/pallas_call | solution.py:441
  11.7 2.6 %collective-permute-start.3 = (f32[8,3328]{1,0:T(8,128)S(1)}, f32[8,3328]{1,0:T(8,128)S(1)}, u32[]{:S(2)}, u32[]{:S(2)}) collective-permute-start(f32[8,3328]{1,0:T(8,128)S(1)} %get-tuple-element.49), channel_id=1, source_target_pairs={{0,2},{1,3},{2,0},{3,1},{4,6},{5,7},{6,4},{7,5},{8,10},{9,11},{10,... | collective-permute-start | bytes 319496 | tf_op jit(solution)/shard_map/ppermute | solution.py:406
  15.4 2.1 %shard_map.79 = (bf16[512,512]{1,0:T(8,128)(2,1)S(1)}, bf16[256,512]{1,0:T(8,128)(2,1)S(1)}, bf16[256,512]{1,0:T(8,128)(2,1)S(1)}, bf16[256,512]{1,0:T(8,128)(2,1)S(1)}) custom-call(s32[2]{0:T(128)S(1)} %pad_add_fusion.j_ref.at_ref, bf16[160,5760]{1,0:T(8,128)(2,1)S(1)} %copy-done.7), custom_call_target="tpu_custom_call" | custom-call | tf_op jit(solution)/shard_map/pallas_call | solution.py:456
  19.6 6.7 %shard_map.80.acc_ref = f32[160,4096]{1,0:T(8,128)S(1)} custom-call(bf16[512,512]{1,0:T(8,128)(2,1)S(1)} %get-tuple-element.52.k_ref, bf16[160,4096]{1,0:T(8,128)(2,1)S(1)} %copy-done.3), custom_call_target="tpu_custom_call" | custom-call | tf_op jit(solution)/shard_map/pallas_call | solution.py:464
  26.3 1.5 copy-done.5
  27.8 1.4 shard_map.81
  29.2 6.4 %all-to-all-start = ((f32[8,8,1280]{2,1,0:T(8,128)}), f32[8,8,1280]{2,1,0:T(8,128)S(1)}, u32[]{:S(2)}, u32[]{:S(2)}) async-start(f32[8,8,1280]{2,1,0:T(8,128)} %shard_map.81), calls=%async_computation | async-start | bytes 655360 | tf_op jit(solution)/shard_map/all_to_all | solution.py:425
  36.0 2.3 %collective-permute-start.6 = (bf16[80,4096]{1,0:T(8,128)(2,1)}, bf16[80,4096]{1,0:T(8,128)(2,1)}, u32[]{:S(2)}, u32[]{:S(2)}) collective-permute-start(bf16[80,4096]{1,0:T(8,128)(2,1)} %get-tuple-element.57), channel_id=1, source_target_pairs={{0,3},{1,0},{2,1},{3,2},{4,7},{5,4},{6,5},{7,6},{8,11},{9,8},{10,9... | collective-permute-start | bytes 1966088 | tf_op jit(solution)/shard_map/ppermute | solution.py:406
  38.3 4.4 %all-to-all-done.got = f32[8,8,1280]{2,1,0:T(8,128)S(1)} async-done(((f32[8,8,1280]{2,1,0:T(8,128)}), f32[8,8,1280]{2,1,0:T(8,128)S(1)}, u32[]{:S(2)}, u32[]{:S(2)}) %all-to-all-start) | async-done | bytes 327712 | tf_op jit(solution)/shard_map/all_to_all | solution.py:425
  43.9 2.3 %collective-permute-start.8 = (bf16[80,4096]{1,0:T(8,128)(2,1)}, bf16[80,4096]{1,0:T(8,128)(2,1)}, u32[]{:S(2)}, u32[]{:S(2)}) collective-permute-start(bf16[80,4096]{1,0:T(8,128)(2,1)} %collective-permute-done.1.grb), channel_id=1, source_target_pairs={{0,3},{1,0},{2,1},{3,2},{4,7},{5,4},{6,5},{7,6},{8,11},{9,8},{10,9... | collective-permute-start | bytes 1966088 | tf_op jit(solution)/shard_map/ppermute | solution.py:406
  46.1 8.2 %all-to-all-start.1 = ((f32[8,8,1280]{2,1,0:T(8,128)}), f32[8,8,1280]{2,1,0:T(8,128)S(1)}, u32[]{:S(2)}, u32[]{:S(2)}) async-start(f32[8,8,1280]{2,1,0:T(8,128)} %shard_map.82), calls=%async_computation.1 | async-start | bytes 655360 | tf_op jit(solution)/shard_map/all_to_all | solution.py:425
  55.5 9.9 %all-to-all-done.1.s_ref = f32[8,8,1280]{2,1,0:T(8,128)S(1)} async-done(((f32[8,8,1280]{2,1,0:T(8,128)}), f32[8,8,1280]{2,1,0:T(8,128)S(1)}, u32[]{:S(2)}, u32[]{:S(2)}) %all-to-all-start.1) | async-done | bytes 327712 | tf_op jit(solution)/shard_map/all_to_all | solution.py:425
  66.0 1.5 collective-permute-done.7.ga
  67.5 10.5 %all_to_all.20.blocks = f32[4,8,3328]{2,1,0:T(8,128)S(1)} all-to-all(f32[4,8,3328]{2,1,0:T(8,128)S(1)} %shard_map.83), channel_id=1, replica_groups=mesh['dp'=64,'chan'=4] {'chan'}, dimensions={0} | all-to-all | bytes 851968 | tf_op jit(solution)/shard_map/all_to_all | solution.py:485
  79.5 2.0 %copy-done.1 = f32[1,160,5760]{2,1,0:T(8,128)S(1)} copy-done((f32[1,160,5760]{2,1,0:T(8,128)S(1)}, f32[1,160,5760]{2,1,0:T(8,128)}, u32[]{:S(2)}) %copy-start.1) | copy-done | bytes 3686424
  81.5 2.4 %shard_map.84 = (f32[64,640]{1,0:T(8,128)S(1)}, f32[64,8,128]{2,1,0:T(8,128)S(1)}) custom-call(f32[4,8,3328]{2,1,0:T(8,128)S(1)} %all_to_all.20.blocks, f32[160,5760]{1,0:T(8,128)S(1)} %bitcast.10, bf16[160,4096]{1,0:T(8,128)(2,1)S(1)} %copy-done.3), custom_call_target="tpu_custom_call" | custom-call | tf_op jit(solution)/shard_map/pallas_call | solution.py:490
  85.3 14.2 %all-to-all-start.3 = ((f32[64,8,128]{2,1,0:T(8,128)}), f32[64,8,128]{2,1,0:T(8,128)S(1)}, u32[]{:S(2)}, u32[]{:S(2)}) async-start(f32[64,8,128]{2,1,0:T(8,128)} %copy-done.10), calls=%async_computation.3 | async-start | bytes 524288 | tf_op jit(solution)/shard_map/all_to_all | solution.py:498
  99.9 3.0 %collective-permute-start.12 = (bf16[256,512]{1,0:T(8,128)(2,1)}, bf16[256,512]{1,0:T(8,128)(2,1)S(1)}, u32[]{:S(2)}, u32[]{:S(2)}) collective-permute-start(bf16[256,512]{1,0:T(8,128)(2,1)} %copy-done.15), channel_id=1, source_target_pairs={{0,2},{1,3},{2,0},{3,1},{4,6},{5,7},{6,4},{7,5},{8,10},{9,11},{10,... | collective-permute-start | bytes 786440 | tf_op jit(solution)/shard_map/ppermute | solution.py:406
  102.9 5.6 %collective-permute-done.11 = bf16[256,512]{1,0:T(8,128)(2,1)S(1)} collective-permute-done((bf16[256,512]{1,0:T(8,128)(2,1)}, bf16[256,512]{1,0:T(8,128)(2,1)S(1)}, u32[]{:S(2)}, u32[]{:S(2)}) %collective-permute-start.11) | collective-permute-done | bytes 262176 | tf_op jit(solution)/shard_map/ppermute | solution.py:406
  108.4 6.2 %collective-permute-done.12 = bf16[256,512]{1,0:T(8,128)(2,1)S(1)} collective-permute-done((bf16[256,512]{1,0:T(8,128)(2,1)}, bf16[256,512]{1,0:T(8,128)(2,1)S(1)}, u32[]{:S(2)}, u32[]{:S(2)}) %collective-permute-start.12) | collective-permute-done | bytes 262176 | tf_op jit(solution)/shard_map/ppermute | solution.py:406
  115.4 1.2 pad_maximum_fusion.mine_ref
  116.6 1.4 collective-permute-start.14
  118.0 2.7 %collective-permute-start.16 = (bf16[80,4096]{1,0:T(8,128)(2,1)}, bf16[80,4096]{1,0:T(8,128)(2,1)S(1)}, u32[]{:S(2)}, u32[]{:S(2)}) collective-permute-start(bf16[80,4096]{1,0:T(8,128)(2,1)} %get-tuple-element.65), channel_id=1, source_target_pairs={{0,3},{1,0},{2,1},{3,2},{4,7},{5,4},{6,5},{7,6},{8,11},{9,8},{10,9... | collective-permute-start | bytes 1966088 | tf_op jit(solution)/shard_map/ppermute | solution.py:406
  120.7 2.7 %collective-permute-start.18 = (bf16[80,4096]{1,0:T(8,128)(2,1)}, bf16[80,4096]{1,0:T(8,128)(2,1)S(1)}, u32[]{:S(2)}, u32[]{:S(2)}) collective-permute-start(bf16[80,4096]{1,0:T(8,128)(2,1)} %collective-permute-done.10.xrb), channel_id=1, source_target_pairs={{0,3},{1,0},{2,1},{3,2},{4,7},{5,4},{6,5},{7,6},{8,11},{9,8},{10,9... | collective-permute-start | bytes 1966088 | tf_op jit(solution)/shard_map/ppermute | solution.py:406
  123.4 1.7 %copy-done.6 = f32[160,4096]{1,0:T(8,128)S(1)} copy-done((f32[160,4096]{1,0:T(8,128)S(1)}, f32[160,4096]{1,0:T(8,128)}, u32[]{:S(2)}) %copy-start.6) | copy-done | bytes 2621464
  125.1 16.3 %shard_map.85 = bf16[160,4096]{1,0:T(8,128)(2,1)} custom-call(s32[2]{0:T(128)S(1)} %pad_add_fusion.j_ref.at_ref, bf16[3,256,512]{2,1,0:T(8,128)(2,1)S(1)} %pad_maximum_fusion.mine_ref, bf16[3,256,512]{2,1,0:T(8,128)(2,1)S(1)} %collective-permute-done.14.other_ref, bf16[80,4096]{1,0:T(8,128)(2,1)S(1)} %copy-done.9, ...), custom_call_target="tpu_custom_call" | custom-call | tf_op jit(solution)/shard_map/pallas_call | solution.py:504
  141.5 8.3 %collective-permute-done.17.xa = bf16[80,4096]{1,0:T(8,128)(2,1)S(1)} collective-permute-done((bf16[80,4096]{1,0:T(8,128)(2,1)}, bf16[80,4096]{1,0:T(8,128)(2,1)S(1)}, u32[]{:S(2)}, u32[]{:S(2)}) %collective-permute-start.17) | collective-permute-done | bytes 655392 | tf_op jit(solution)/shard_map/ppermute | solution.py:406
  149.8 18.7 %shard_map.86 = (f32[160,5760]{1,0:T(8,128)}, f32[160,4]{1,0:T(8,128)S(1)}) custom-call(s32[2]{0:T(128)S(1)} %pad_add_fusion.j_ref.at_ref, bf16[160,4096]{1,0:T(8,128)(2,1)S(1)} %copy-done.4, bf16[80,4096]{1,0:T(8,128)(2,1)} %collective-permute-done.9.xlt, bf16[80,4096]{1,0:T(8,128)(2,1)S(1)} %collective-permute-done.15.xlb, ...), custom_call_target="tpu_custom_call" | custom-call | tf_op jit(solution)/shard_map/pallas_call | solution.py:513
  (65 shorter events, 13.1 us)
Async XLA Ops:
  1.9 4.8 %copy-start.3 = (bf16[160,4096]{1,0:T(8,128)(2,1)S(1)}, bf16[160,4096]{1,0:T(8,128)(2,1)}, u32[]{:S(2)}) copy-start(bf16[160,4096]{1,0:T(8,128)(2,1)} %g_ref.5) | copy-start | bytes 3932164
  3.1 24.7 %collective-permute-start = (bf16[80,4096]{1,0:T(8,128)(2,1)}, bf16[80,4096]{1,0:T(8,128)(2,1)S(1)}, u32[]{:S(2)}, u32[]{:S(2)}) collective-permute-start(bf16[80,4096]{1,0:T(8,128)(2,1)} %get-tuple-element.57), channel_id=1, source_target_pairs={{0,1},{1,2},{2,3},{3,0},{4,5},{5,6},{6,7},{7,4},{8,9},{9,10},{10,1... | collective-permute-start | bytes 1966088 | tf_op jit(solution)/shard_map/ppermute | solution.py:406
  5.2 22.6 %collective-permute-start.1 = (bf16[80,4096]{1,0:T(8,128)(2,1)}, bf16[80,4096]{1,0:T(8,128)(2,1)}, u32[]{:S(2)}, u32[]{:S(2)}) collective-permute-start(bf16[80,4096]{1,0:T(8,128)(2,1)} %get-tuple-element.56), channel_id=1, source_target_pairs={{0,3},{1,0},{2,1},{3,2},{4,7},{5,4},{6,5},{7,6},{8,11},{9,8},{10,9... | collective-permute-start | bytes 1966088 | tf_op jit(solution)/shard_map/ppermute | solution.py:406
  6.7 2.0 %copy-start = (f32[1,160,5760]{2,1,0:T(8,128)S(1)}, f32[1,160,5760]{2,1,0:T(8,128)}, u32[]{:S(2)}) copy-start(f32[1,160,5760]{2,1,0:T(8,128)} %param.8) | copy-start | bytes 11059204
  9.5 6.0 %copy-start.7 = (bf16[160,5760]{1,0:T(8,128)(2,1)S(1)}, bf16[160,5760]{1,0:T(8,128)(2,1)}, u32[]{:S(2)}) copy-start(bf16[160,5760]{1,0:T(8,128)(2,1)} %k_ref) | copy-start | bytes 5529604
  11.6 16.1 %collective-permute-start.2 = (f32[8,3328]{1,0:T(8,128)S(1)}, f32[8,3328]{1,0:T(8,128)S(1)}, u32[]{:S(2)}, u32[]{:S(2)}) collective-permute-start(f32[8,3328]{1,0:T(8,128)S(1)} %get-tuple-element.48), channel_id=1, source_target_pairs={{0,1},{1,2},{2,3},{3,0},{4,5},{5,6},{6,7},{7,4},{8,9},{9,10},{10,1... | collective-permute-start | bytes 319496 | tf_op jit(solution)/shard_map/ppermute | solution.py:406
  11.7 16.1 %collective-permute-start.3 = (f32[8,3328]{1,0:T(8,128)S(1)}, f32[8,3328]{1,0:T(8,128)S(1)}, u32[]{:S(2)}, u32[]{:S(2)}) collective-permute-start(f32[8,3328]{1,0:T(8,128)S(1)} %get-tuple-element.49), channel_id=1, source_target_pairs={{0,2},{1,3},{2,0},{3,1},{4,6},{5,7},{6,4},{7,5},{8,10},{9,11},{10,... | collective-permute-start | bytes 319496 | tf_op jit(solution)/shard_map/ppermute | solution.py:406
  14.4 13.4 %collective-permute-start.4 = (f32[8,3328]{1,0:T(8,128)S(1)}, f32[8,3328]{1,0:T(8,128)S(1)}, u32[]{:S(2)}, u32[]{:S(2)}) collective-permute-start(f32[8,3328]{1,0:T(8,128)S(1)} %get-tuple-element.50), channel_id=1, source_target_pairs={{0,3},{1,0},{2,1},{3,2},{4,7},{5,4},{6,5},{7,6},{8,11},{9,8},{10,9... | collective-permute-start | bytes 319496 | tf_op jit(solution)/shard_map/ppermute | solution.py:406
  19.6 8.2 %copy-start.4 = (bf16[160,4096]{1,0:T(8,128)(2,1)S(1)}, bf16[160,4096]{1,0:T(8,128)(2,1)}, u32[]{:S(2)}) copy-start(bf16[160,4096]{1,0:T(8,128)(2,1)} %x0.1) | copy-start | bytes 3932164
  26.3 1.5 copy-start.5
  29.2 13.5 %all-to-all-start = ((f32[8,8,1280]{2,1,0:T(8,128)}), f32[8,8,1280]{2,1,0:T(8,128)S(1)}, u32[]{:S(2)}, u32[]{:S(2)}) async-start(f32[8,8,1280]{2,1,0:T(8,128)} %shard_map.81), calls=%async_computation | async-start | bytes 655360 | tf_op jit(solution)/shard_map/all_to_all | solution.py:425
  35.6 19.9 %collective-permute-start.5 = (bf16[80,4096]{1,0:T(8,128)(2,1)}, bf16[80,4096]{1,0:T(8,128)(2,1)}, u32[]{:S(2)}, u32[]{:S(2)}) collective-permute-start(bf16[80,4096]{1,0:T(8,128)(2,1)} %get-tuple-element.56), channel_id=1, source_target_pairs={{0,1},{1,2},{2,3},{3,0},{4,5},{5,6},{6,7},{7,4},{8,9},{9,10},{10,1... | collective-permute-start | bytes 1966088 | tf_op jit(solution)/shard_map/ppermute | solution.py:406
  36.0 19.5 %collective-permute-start.6 = (bf16[80,4096]{1,0:T(8,128)(2,1)}, bf16[80,4096]{1,0:T(8,128)(2,1)}, u32[]{:S(2)}, u32[]{:S(2)}) collective-permute-start(bf16[80,4096]{1,0:T(8,128)(2,1)} %get-tuple-element.57), channel_id=1, source_target_pairs={{0,3},{1,0},{2,1},{3,2},{4,7},{5,4},{6,5},{7,6},{8,11},{9,8},{10,9... | collective-permute-start | bytes 1966088 | tf_op jit(solution)/shard_map/ppermute | solution.py:406
  43.5 24.1 %collective-permute-start.7 = (bf16[80,4096]{1,0:T(8,128)(2,1)}, bf16[80,4096]{1,0:T(8,128)(2,1)}, u32[]{:S(2)}, u32[]{:S(2)}) collective-permute-start(bf16[80,4096]{1,0:T(8,128)(2,1)} %copy-done.8), channel_id=1, source_target_pairs={{0,1},{1,2},{2,3},{3,0},{4,5},{5,6},{6,7},{7,4},{8,9},{9,10},{10,1... | collective-permute-start | bytes 1966088 | tf_op jit(solution)/shard_map/ppermute | solution.py:406
  43.9 23.7 %collective-permute-start.8 = (bf16[80,4096]{1,0:T(8,128)(2,1)}, bf16[80,4096]{1,0:T(8,128)(2,1)}, u32[]{:S(2)}, u32[]{:S(2)}) collective-permute-start(bf16[80,4096]{1,0:T(8,128)(2,1)} %collective-permute-done.1.grb), channel_id=1, source_target_pairs={{0,3},{1,0},{2,1},{3,2},{4,7},{5,4},{6,5},{7,6},{8,11},{9,8},{10,9... | collective-permute-start | bytes 1966088 | tf_op jit(solution)/shard_map/ppermute | solution.py:406
  46.1 19.3 %all-to-all-start.1 = ((f32[8,8,1280]{2,1,0:T(8,128)}), f32[8,8,1280]{2,1,0:T(8,128)S(1)}, u32[]{:S(2)}, u32[]{:S(2)}) async-start(f32[8,8,1280]{2,1,0:T(8,128)} %shard_map.82), calls=%async_computation.1 | async-start | bytes 655360 | tf_op jit(solution)/shard_map/all_to_all | solution.py:425
  78.0 37.3 %collective-permute-start.10 = (bf16[80,4096]{1,0:T(8,128)(2,1)}, bf16[80,4096]{1,0:T(8,128)(2,1)}, u32[]{:S(2)}, u32[]{:S(2)}) collective-permute-start(bf16[80,4096]{1,0:T(8,128)(2,1)} %get-tuple-element.66), channel_id=1, source_target_pairs={{0,3},{1,0},{2,1},{3,2},{4,7},{5,4},{6,5},{7,6},{8,11},{9,8},{10,9... | collective-permute-start | bytes 1966088 | tf_op jit(solution)/shard_map/ppermute | solution.py:406
  78.9 36.5 %collective-permute-start.9 = (bf16[80,4096]{1,0:T(8,128)(2,1)}, bf16[80,4096]{1,0:T(8,128)(2,1)}, u32[]{:S(2)}, u32[]{:S(2)}) collective-permute-start(bf16[80,4096]{1,0:T(8,128)(2,1)} %get-tuple-element.65), channel_id=1, source_target_pairs={{0,1},{1,2},{2,3},{3,0},{4,5},{5,6},{6,7},{7,4},{8,9},{9,10},{10,1... | collective-permute-start | bytes 1966088 | tf_op jit(solution)/shard_map/ppermute | solution.py:406
  79.5 2.0 %copy-start.1 = (f32[1,160,5760]{2,1,0:T(8,128)S(1)}, f32[1,160,5760]{2,1,0:T(8,128)}, u32[]{:S(2)}) copy-start(f32[1,160,5760]{2,1,0:T(8,128)} %param.8) | copy-start | bytes 11059204
  85.3 38.1 %copy-start.9 = (bf16[80,4096]{1,0:T(8,128)(2,1)S(1)}, bf16[80,4096]{1,0:T(8,128)(2,1)}, u32[]{:S(2)}) copy-start(bf16[80,4096]{1,0:T(8,128)(2,1)} %copy-done.8) | copy-start | bytes 1966084
  85.3 30.1 %all-to-all-start.3 = ((f32[64,8,128]{2,1,0:T(8,128)}), f32[64,8,128]{2,1,0:T(8,128)S(1)}, u32[]{:S(2)}, u32[]{:S(2)}) async-start(f32[64,8,128]{2,1,0:T(8,128)} %copy-done.10), calls=%async_computation.3 | async-start | bytes 524288 | tf_op jit(solution)/shard_map/all_to_all | solution.py:498
  99.5 8.9 %collective-permute-start.11 = (bf16[256,512]{1,0:T(8,128)(2,1)}, bf16[256,512]{1,0:T(8,128)(2,1)S(1)}, u32[]{:S(2)}, u32[]{:S(2)}) collective-permute-start(bf16[256,512]{1,0:T(8,128)(2,1)} %copy-done.16), channel_id=1, source_target_pairs={{0,1},{1,2},{2,3},{3,0},{4,5},{5,6},{6,7},{7,4},{8,9},{9,10},{10,1... | collective-permute-start | bytes 786440 | tf_op jit(solution)/shard_map/ppermute | solution.py:406
  99.9 14.8 %collective-permute-start.12 = (bf16[256,512]{1,0:T(8,128)(2,1)}, bf16[256,512]{1,0:T(8,128)(2,1)S(1)}, u32[]{:S(2)}, u32[]{:S(2)}) collective-permute-start(bf16[256,512]{1,0:T(8,128)(2,1)} %copy-done.15), channel_id=1, source_target_pairs={{0,2},{1,3},{2,0},{3,1},{4,6},{5,7},{6,4},{7,5},{8,10},{9,11},{10,... | collective-permute-start | bytes 786440 | tf_op jit(solution)/shard_map/ppermute | solution.py:406
  102.9 12.5 %collective-permute-start.13 = (bf16[256,512]{1,0:T(8,128)(2,1)}, bf16[256,512]{1,0:T(8,128)(2,1)}, u32[]{:S(2)}, u32[]{:S(2)}) collective-permute-start(bf16[256,512]{1,0:T(8,128)(2,1)} %copy-done.14), channel_id=1, source_target_pairs={{0,3},{1,0},{2,1},{3,2},{4,7},{5,4},{6,5},{7,6},{8,11},{9,8},{10,9... | collective-permute-start | bytes 786440 | tf_op jit(solution)/shard_map/ppermute | solution.py:406
  108.4 6.2 %copy-start.17 = (bf16[256,512]{1,0:T(8,128)(2,1)}, bf16[256,512]{1,0:T(8,128)(2,1)S(1)}, u32[]{:S(2)}) copy-start(bf16[256,512]{1,0:T(8,128)(2,1)S(1)} %collective-permute-done.11) | copy-start | bytes 786436
  115.4 34.4 %copy-start.12 = (f32[64,640]{1,0:T(8,128)S(1)}, f32[64,640]{1,0:T(8,128)}, u32[]{:S(2)}) copy-start(f32[64,640]{1,0:T(8,128)} %copy-done.11) | copy-start | bytes 491524
  116.6 6.8 %collective-permute-start.14 = (bf16[3,256,512]{2,1,0:T(8,128)(2,1)S(1)}, bf16[3,256,512]{2,1,0:T(8,128)(2,1)S(1)}, u32[]{:S(2)}, u32[]{:S(2)}) collective-permute-start(bf16[3,256,512]{2,1,0:T(8,128)(2,1)S(1)} %pad_maximum_fusion.mine_ref), channel_id=1, source_target_pairs={{0,4},{4,0},{8,12},{12,8},{16,20},{20,16},{24,28},{28,24},{32,36},... | collective-permute-start | bytes 2359304 | tf_op jit(solution)/shard_map/ppermute | solution.py:501
  118.0 23.5 %collective-permute-start.15 = (bf16[80,4096]{1,0:T(8,128)(2,1)}, bf16[80,4096]{1,0:T(8,128)(2,1)S(1)}, u32[]{:S(2)}, u32[]{:S(2)}) collective-permute-start(bf16[80,4096]{1,0:T(8,128)(2,1)} %get-tuple-element.66), channel_id=1, source_target_pairs={{0,1},{1,2},{2,3},{3,0},{4,5},{5,6},{6,7},{7,4},{8,9},{9,10},{10,1... | collective-permute-start | bytes 1966088 | tf_op jit(solution)/shard_map/ppermute | solution.py:406
  118.0 23.5 %collective-permute-start.16 = (bf16[80,4096]{1,0:T(8,128)(2,1)}, bf16[80,4096]{1,0:T(8,128)(2,1)S(1)}, u32[]{:S(2)}, u32[]{:S(2)}) collective-permute-start(bf16[80,4096]{1,0:T(8,128)(2,1)} %get-tuple-element.65), channel_id=1, source_target_pairs={{0,3},{1,0},{2,1},{3,2},{4,7},{5,4},{6,5},{7,6},{8,11},{9,8},{10,9... | collective-permute-start | bytes 1966088 | tf_op jit(solution)/shard_map/ppermute | solution.py:406
  120.7 29.1 %collective-permute-start.17 = (bf16[80,4096]{1,0:T(8,128)(2,1)}, bf16[80,4096]{1,0:T(8,128)(2,1)S(1)}, u32[]{:S(2)}, u32[]{:S(2)}) collective-permute-start(bf16[80,4096]{1,0:T(8,128)(2,1)} %collective-permute-done.9.xlt), channel_id=1, source_target_pairs={{0,1},{1,2},{2,3},{3,0},{4,5},{5,6},{6,7},{7,4},{8,9},{9,10},{10,1... | collective-permute-start | bytes 1966088 | tf_op jit(solution)/shard_map/ppermute | solution.py:406
  120.7 29.1 %collective-permute-start.18 = (bf16[80,4096]{1,0:T(8,128)(2,1)}, bf16[80,4096]{1,0:T(8,128)(2,1)S(1)}, u32[]{:S(2)}, u32[]{:S(2)}) collective-permute-start(bf16[80,4096]{1,0:T(8,128)(2,1)} %collective-permute-done.10.xrb), channel_id=1, source_target_pairs={{0,3},{1,0},{2,1},{3,2},{4,7},{5,4},{6,5},{7,6},{8,11},{9,8},{10,9... | collective-permute-start | bytes 1966088 | tf_op jit(solution)/shard_map/ppermute | solution.py:406
  123.4 1.7 %copy-start.6 = (f32[160,4096]{1,0:T(8,128)S(1)}, f32[160,4096]{1,0:T(8,128)}, u32[]{:S(2)}) copy-start(f32[160,4096]{1,0:T(8,128)} %copy-done.5) | copy-start | bytes 7864324
  (9 other events, 7.6 us)
where the time goes:
time: 170 us; the launch traced here: 169 us
  Pallas kernels  53.3 us (31%)
  starting transfers between devices  53.1 us (31%)
  waiting for transfers between devices  36 us (21%)
  local copies, waits for them, and re-layouts  14.2 us (8%)
  blocking collectives  10.5 us (6%)
    ppermute x18, starting transfers between devices, around(): return lax.ppermute(array, 'chan', [(i, (i + s) % 4) for i in range(4)])  22.9 us
    ppermute x18, waiting for transfers between devices, around(): return lax.ppermute(array, 'chan', [(i, (i + s) % 4) for i in range(4)])  21.7 us
    pallas_call x1, Pallas kernels, per_device(): call(weight_kernel, [sds((ch, TAPS * 640), F32), sds((ch, 4), F32)], [plt...  18.7 us
    pallas_call x1, Pallas kernels, per_device(): call(rest_kernel, sds((ch, CELLS), BF16), [pltpu.VMEM((3, SIDE, SIDE), BF...  16.3 us
    all_to_all x2, starting transfers between devices, exchanged(): lax.all_to_all(array, 'dp', 0, 0, axis_index_groups=line_groups(axis), ti...  14.6 us
    all_to_all x2, waiting for transfers between devices, exchanged(): lax.all_to_all(array, 'dp', 0, 0, axis_index_groups=line_groups(axis), ti...  14.3 us
    all_to_all x1, starting transfers between devices, per_device(): q_got = lax.all_to_all(q_part, 'dp', 0, 0, tiled=True)  14.2 us
    unnamed x39, local copies, waits for them, and re-layouts  14.2 us
  transfers between devices with their start and end apart: 22, of which 6 were waited for; matrix products, arithmetic and copies ran while one was open for 0% of the time, Pallas kernels for 19%

commit v1 on v0

--- a/solution.py
+++ b/solution.py
@@ -472,21 +472,23 @@
     )(sent[0], *got, x)
     part, gb, gt = lax.optimization_barrier((part, gb, gt))
     glb, grt = around(gb, 1), around(gt, 3)
-    part = exchanged(part, "xc")
+    part = after(exchanged(part, "xc"), glb, grt)
     part = call(total_kernel, group, (), 0, 1, 8)(part)
-    glt, grb, part = lax.optimization_barrier((glt, grb, part))
+    glt, grb, part, *k_sent = lax.optimization_barrier((glt, grb, part, *k_sent))
+    k_got = [around(v, s) for s, v in zip((1, 2, 3), k_sent, strict=True)]
     ga, go = around(glt, 1), around(grb, 3)
-    part = after(exchanged(part, "z"), glb, grt)
+    part = exchanged(part, "z")
     mine = call(
         functools.partial(image_kernel, 1.0 / workers), sds((4, 8, PAY), F32), [pltpu.VMEM((40, CELLS), F32)], 0, 2, 16
     )(part, x)
     xt, xb = cut(x)
-    mine = after(mine, ga, go, xt, xb)
+    mine, *k_got = lax.optimization_barrier((mine, *k_got, ga, go, xt, xb))[:4]
+    k_mine = jnp.stack(k_got)
+    k_other = lax.ppermute(k_mine, "dp", [(i, i ^ 1) for i in range(workers)])
     theirs = lax.all_to_all(mine, "chan", 0, 0, tiled=True)
-    xt, xb, theirs, *k_sent = lax.optimization_barrier((xt, xb, theirs, *k_sent))
+    xt, xb, theirs = lax.optimization_barrier((xt, xb, theirs))
     xlt, xrb = around(xt, 1), around(xb, 3)
     xlb, xrt = around(xb, 1), around(xt, 3)
-    k_got = [around(v, s) for s, v in zip((1, 2, 3), k_sent, strict=True)]
     basis, q_part = call(
         factor_kernel,
         [sds((64, 640), F32), sds((workers, 8, 128), F32)],
@@ -496,9 +498,7 @@
         16,
     )(theirs, err, g)
     q_got = lax.all_to_all(q_part, "dp", 0, 0, tiled=True)
-    xlt, xrb, q_got, *k_got = lax.optimization_barrier((xlt, xrb, q_got, *k_got))
-    k_mine = jnp.stack(k_got)
-    k_other = lax.ppermute(k_mine, "dp", [(i, i ^ 1) for i in range(workers)])
+    xlt, xrb, q_got = lax.optimization_barrier((xlt, xrb, q_got))
     xa, xo = around(xlt, 1), around(xrb, 3)
 
     in_grad = call(

time: 170 us -> 165 us (0.971)
  waiting for transfers between devices: 36 us -> 18.6 us
  blocking collectives: 10.5 us -> 25 us
  starting transfers between devices: 53.1 us -> 49.3 us
  local copies, waits for them, and re-layouts: 14.2 us -> 15.9 us
    ppermute x18, waiting for transfers between devices: 21.7 us -> 5.03 us  [around(): return lax.ppermute(array, 'chan', [(i, (i + s) % 4) for i in range(4)])]
    all_to_all x0 -> x1, blocking collectives: none -> 14.2 us  [exchanged(): lax.all_to_all(array, 'dp', 0, 0, axis_index_groups=line_groups(axis), ti...]
    all_to_all x2 -> x1, waiting for transfers between devices: 14.3 us -> 6.14 us  [exchanged(): lax.all_to_all(array, 'dp', 0, 0, axis_index_groups=line_groups(axis), ti...]
    all_to_all x1, waiting for transfers between devices: 0.01 us -> 7.41 us  [per_device(): q_got = lax.all_to_all(q_part, 'dp', 0, 0, tiled=True)]
    all_to_all x2 -> x1, starting transfers between devices: 14.6 us -> 8.19 us  [exchanged(): lax.all_to_all(array, 'dp', 0, 0, axis_index_groups=line_groups(axis), ti...]
    all_to_all x1, starting transfers between devices: 14.2 us -> 17 us  [per_device(): q_got = lax.all_to_all(q_part, 'dp', 0, 0, tiled=True)]
    unnamed x39 -> x37, local copies, waits for them, and re-layouts: 14.2 us -> 15.9 us
  transfers between devices with their start and end apart: 22 -> 21, of which waited for: 6 -> 5; matrix products, arithmetic and copies ran while one was open for 0% -> 1% of each run, Pallas kernels for 19% -> 20%
where the time goes in v1:
time: 165 us; the launch traced here: 164 us
  Pallas kernels  53.6 us (32%)
  starting transfers between devices  49.3 us (30%)
  blocking collectives  25 us (15%)
  waiting for transfers between devices  18.6 us (11%)
  local copies, waits for them, and re-layouts  15.9 us (10%)
    ppermute x18, starting transfers between devices, around(): return lax.ppermute(array, 'chan', [(i, (i + s) % 4) for i in range(4)])  23.5 us
    pallas_call x1, Pallas kernels, per_device(): call(weight_kernel, [sds((ch, TAPS * 640), F32), sds((ch, 4), F32)], [plt...  19.1 us
    all_to_all x1, starting transfers between devices, per_device(): q_got = lax.all_to_all(q_part, 'dp', 0, 0, tiled=True)  17 us
    pallas_call x1, Pallas kernels, per_device(): call(rest_kernel, sds((ch, CELLS), BF16), [pltpu.VMEM((3, SIDE, SIDE), BF...  16.4 us
    unnamed x37, local copies, waits for them, and re-layouts  15.9 us
    all_to_all x1, blocking collectives, exchanged(): lax.all_to_all(array, 'dp', 0, 0, axis_index_groups=line_groups(axis), ti...  14.2 us
    all_to_all x1, blocking collectives, per_device(): theirs = lax.all_to_all(mine, 'chan', 0, 0, tiled=True)  10.7 us
    all_to_all x1, starting transfers between devices, exchanged(): lax.all_to_all(array, 'dp', 0, 0, axis_index_groups=line_groups(axis), ti...  8.19 us
  transfers between devices with their start and end apart: 21, of which 5 were waited for; matrix products, arithmetic and copies ran while one was open for 1% of the time, Pallas kernels for 20%

profile of v1, /device:TPU:1, one launch (start us, length us, event | category | flops | bytes accessed | tf_op | source)
XLA Modules:
  0.0 164.4 jit_solution(3721444325946479850)
XLA Ops:
  0.6 1.3 copy-done.2
  2.9 2.1 %collective-permute-start = (bf16[80,4096]{1,0:T(8,128)(2,1)S(1)}, bf16[80,4096]{1,0:T(8,128)(2,1)}, u32[]{:S(2)}, u32[]{:S(2)}) collective-permute-start(bf16[80,4096]{1,0:T(8,128)(2,1)S(1)} %get-tuple-element.56), channel_id=1, source_target_pairs={{0,1},{1,2},{2,3},{3,0},{4,5},{5,6},{6,7},{7,4},{8,9},{9,10},{10,1... | collective-permute-start | bytes 1966088 | tf_op jit(solution)/shard_map/ppermute | solution.py:406
  5.0 1.4 collective-permute-start.1
  6.5 2.0 %copy-done = f32[1,160,5760]{2,1,0:T(8,128)S(1)} copy-done((f32[1,160,5760]{2,1,0:T(8,128)S(1)}, f32[1,160,5760]{2,1,0:T(8,128)}, u32[]{:S(2)}) %copy-start) | copy-done | bytes 3686424
  9.2 2.2 %shard_map.78 = (f32[8,3328]{1,0:T(8,128)S(1)}, f32[8,3328]{1,0:T(8,128)S(1)}, f32[8,3328]{1,0:T(8,128)S(1)}, f32[8,3328]{1,0:T(8,128)S(1)}) custom-call(s32[2]{0:T(128)S(1)} %pad_add_fusion.j_ref.at_ref, f32[4,160]{1,0:T(4,128)S(1)} %bitcast.11, bf16[160,4096]{1,0:T(8,128)(2,1)S(1)} %copy-done.3, f32[160,5760]{1,0:T(8,128)S(1)} %bitcast.9), custom_call_target="tpu_custom_call" | custom-call | tf_op jit(solution)/shard_map/pallas_call | solution.py:441
  11.5 2.6 %collective-permute-start.3 = (f32[8,3328]{1,0:T(8,128)S(1)}, f32[8,3328]{1,0:T(8,128)S(1)}, u32[]{:S(2)}, u32[]{:S(2)}) collective-permute-start(f32[8,3328]{1,0:T(8,128)S(1)} %get-tuple-element.49), channel_id=1, source_target_pairs={{0,2},{1,3},{2,0},{3,1},{4,6},{5,7},{6,4},{7,5},{8,10},{9,11},{10,... | collective-permute-start | bytes 319496 | tf_op jit(solution)/shard_map/ppermute | solution.py:406
  15.2 2.1 %shard_map.79 = (bf16[512,512]{1,0:T(8,128)(2,1)S(1)}, bf16[256,512]{1,0:T(8,128)(2,1)S(1)}, bf16[256,512]{1,0:T(8,128)(2,1)S(1)}, bf16[256,512]{1,0:T(8,128)(2,1)S(1)}) custom-call(s32[2]{0:T(128)S(1)} %pad_add_fusion.j_ref.at_ref, bf16[160,5760]{1,0:T(8,128)(2,1)S(1)} %copy-done.7), custom_call_target="tpu_custom_call" | custom-call | tf_op jit(solution)/shard_map/pallas_call | solution.py:456
  18.7 6.7 %shard_map.80.acc_ref = f32[160,4096]{1,0:T(8,128)S(1)} custom-call(bf16[512,512]{1,0:T(8,128)(2,1)S(1)} %get-tuple-element.52.k_ref, bf16[160,4096]{1,0:T(8,128)(2,1)S(1)} %copy-done.3), custom_call_target="tpu_custom_call" | custom-call | tf_op jit(solution)/shard_map/pallas_call | solution.py:464
  25.4 1.5 copy-done.5
  28.0 2.3 %collective-permute-start.6 = (bf16[80,4096]{1,0:T(8,128)(2,1)S(1)}, bf16[80,4096]{1,0:T(8,128)(2,1)S(1)}, u32[]{:S(2)}, u32[]{:S(2)}) collective-permute-start(bf16[80,4096]{1,0:T(8,128)(2,1)S(1)} %get-tuple-element.56), channel_id=1, source_target_pairs={{0,3},{1,0},{2,1},{3,2},{4,7},{5,4},{6,5},{7,6},{8,11},{9,8},{10,9... | collective-permute-start | bytes 1966088 | tf_op jit(solution)/shard_map/ppermute | solution.py:406
  30.3 14.2 %all_to_all.20.got = f32[8,8,1280]{2,1,0:T(8,128)S(1)} all-to-all(f32[8,8,1280]{2,1,0:T(8,128)S(1)} %shard_map.81), channel_id=1, replica_groups={{0,4,64,68,128,132,192,196},{8,12,72,76,136,140,200,204},{16,20,80,84,1..., dimensions={0} | all-to-all | bytes 655360 | tf_op jit(solution)/shard_map/all_to_all | solution.py:425
  46.9 2.7 %collective-permute-start.11 = (bf16[80,4096]{1,0:T(8,128)(2,1)}, bf16[80,4096]{1,0:T(8,128)(2,1)}, u32[]{:S(2)}, u32[]{:S(2)}) collective-permute-start(bf16[80,4096]{1,0:T(8,128)(2,1)} %collective-permute-done.1.grb), channel_id=1, source_target_pairs={{0,3},{1,0},{2,1},{3,2},{4,7},{5,4},{6,5},{7,6},{8,11},{9,8},{10,9... | collective-permute-start | bytes 1966088 | tf_op jit(solution)/shard_map/ppermute | solution.py:406
  49.6 8.2 %all-to-all-start.1 = ((f32[8,8,1280]{2,1,0:T(8,128)}), f32[8,8,1280]{2,1,0:T(8,128)S(1)}, u32[]{:S(2)}, u32[]{:S(2)}) async-start(f32[8,8,1280]{2,1,0:T(8,128)} %shard_map.82), calls=%async_computation.1 | async-start | bytes 655360 | tf_op jit(solution)/shard_map/all_to_all | solution.py:425
  57.8 1.2 collective-permute-start.8
  59.0 1.5 collective-permute-start.9
  60.5 1.2 shard_map.76
  61.7 6.1 %all-to-all-done.1.s_ref = f32[8,8,1280]{2,1,0:T(8,128)S(1)} async-done(((f32[8,8,1280]{2,1,0:T(8,128)}), f32[8,8,1280]{2,1,0:T(8,128)S(1)}, u32[]{:S(2)}, u32[]{:S(2)}) %all-to-all-start.1) | async-done | bytes 327712 | tf_op jit(solution)/shard_map/all_to_all | solution.py:425
  68.4 2.5 %collective-permute-done.7 = bf16[256,512]{1,0:T(8,128)(2,1)S(1)} collective-permute-done((bf16[256,512]{1,0:T(8,128)(2,1)}, bf16[256,512]{1,0:T(8,128)(2,1)S(1)}, u32[]{:S(2)}, u32[]{:S(2)}) %collective-permute-start.7) | collective-permute-done | bytes 262176 | tf_op jit(solution)/shard_map/ppermute | solution.py:406
  71.6 1.7 %collective-permute-done.9 = bf16[256,512]{1,0:T(8,128)(2,1)} collective-permute-done((bf16[256,512]{1,0:T(8,128)(2,1)S(1)}, bf16[256,512]{1,0:T(8,128)(2,1)}, u32[]{:S(2)}, u32[]{:S(2)}) %collective-permute-start.9) | collective-permute-done | bytes 262176 | tf_op jit(solution)/shard_map/ppermute | solution.py:406
  73.4 10.7 %all_to_all.21.blocks = f32[4,8,3328]{2,1,0:T(8,128)S(1)} all-to-all(f32[4,8,3328]{2,1,0:T(8,128)S(1)} %shard_map.83), channel_id=1, replica_groups=mesh['dp'=64,'chan'=4] {'chan'}, dimensions={0} | all-to-all | bytes 851968 | tf_op jit(solution)/shard_map/all_to_all | solution.py:488
  84.4 2.4 %collective-permute-start.13 = (bf16[80,4096]{1,0:T(8,128)(2,1)}, bf16[80,4096]{1,0:T(8,128)(2,1)}, u32[]{:S(2)}, u32[]{:S(2)}) collective-permute-start(bf16[80,4096]{1,0:T(8,128)(2,1)} %get-tuple-element.69), channel_id=1, source_target_pairs={{0,3},{1,0},{2,1},{3,2},{4,7},{5,4},{6,5},{7,6},{8,11},{9,8},{10,9... | collective-permute-start | bytes 1966088 | tf_op jit(solution)/shard_map/ppermute | solution.py:406
  86.8 2.0 %copy-done.1 = f32[1,160,5760]{2,1,0:T(8,128)S(1)} copy-done((f32[1,160,5760]{2,1,0:T(8,128)S(1)}, f32[1,160,5760]{2,1,0:T(8,128)}, u32[]{:S(2)}) %copy-start.1) | copy-done | bytes 3686424
  88.8 3.1 %shard_map.84 = (f32[64,640]{1,0:T(8,128)S(1)}, f32[64,8,128]{2,1,0:T(8,128)}) custom-call(f32[4,8,3328]{2,1,0:T(8,128)S(1)} %all_to_all.21.blocks, f32[160,5760]{1,0:T(8,128)S(1)} %bitcast.10, bf16[160,4096]{1,0:T(8,128)(2,1)S(1)} %copy-done.3), custom_call_target="tpu_custom_call" | custom-call | tf_op jit(solution)/shard_map/pallas_call | solution.py:492
  92.6 17.0 %all-to-all-start.3 = ((f32[64,8,128]{2,1,0:T(8,128)}), f32[64,8,128]{2,1,0:T(8,128)}, u32[]{:S(2)}, u32[]{:S(2)}) async-start(f32[64,8,128]{2,1,0:T(8,128)} %get-tuple-element.71), calls=%async_computation.3 | async-start | bytes 524288 | tf_op jit(solution)/shard_map/all_to_all | solution.py:500
  109.6 1.2 pad_maximum_fusion.mine_ref
  111.4 2.7 %collective-permute-start.16 = (bf16[80,4096]{1,0:T(8,128)(2,1)}, bf16[80,4096]{1,0:T(8,128)(2,1)}, u32[]{:S(2)}, u32[]{:S(2)}) collective-permute-start(bf16[80,4096]{1,0:T(8,128)(2,1)} %get-tuple-element.68), channel_id=1, source_target_pairs={{0,3},{1,0},{2,1},{3,2},{4,7},{5,4},{6,5},{7,6},{8,11},{9,8},{10,9... | collective-permute-start | bytes 1966088 | tf_op jit(solution)/shard_map/ppermute | solution.py:406
  114.1 7.4 %all-to-all-done.3.got = f32[64,8,128]{2,1,0:T(8,128)} async-done(((f32[64,8,128]{2,1,0:T(8,128)}), f32[64,8,128]{2,1,0:T(8,128)}, u32[]{:S(2)}, u32[]{:S(2)}) %all-to-all-start.3) | async-done | bytes 262176 | tf_op jit(solution)/shard_map/all_to_all | solution.py:500
  121.5 2.7 %collective-permute-start.18 = (bf16[80,4096]{1,0:T(8,128)(2,1)}, bf16[80,4096]{1,0:T(8,128)(2,1)S(1)}, u32[]{:S(2)}, u32[]{:S(2)}) collective-permute-start(bf16[80,4096]{1,0:T(8,128)(2,1)} %collective-permute-done.13.xrb), channel_id=1, source_target_pairs={{0,3},{1,0},{2,1},{3,2},{4,7},{5,4},{6,5},{7,6},{8,11},{9,8},{10,9... | collective-permute-start | bytes 1966088 | tf_op jit(solution)/shard_map/ppermute | solution.py:406
  124.2 1.7 %copy-done.6 = f32[160,4096]{1,0:T(8,128)S(1)} copy-done((f32[160,4096]{1,0:T(8,128)S(1)}, f32[160,4096]{1,0:T(8,128)}, u32[]{:S(2)}) %copy-start.6) | copy-done | bytes 2621464
  125.9 1.1 copy-done.9
  128.1 16.4 %shard_map.85 = bf16[160,4096]{1,0:T(8,128)(2,1)} custom-call(s32[2]{0:T(128)S(1)} %pad_add_fusion.j_ref.at_ref, bf16[3,256,512]{2,1,0:T(8,128)(2,1)S(1)} %pad_maximum_fusion.mine_ref, bf16[3,256,512]{2,1,0:T(8,128)(2,1)} %collective-permute-done.14.other_ref, bf16[80,4096]{1,0:T(8,128)(2,1)} %collective-permute-done.glt, bf16[80,4096]{1,0:T(8,128)(2,1)S(1)} %copy-done.9, ...), custom_call_target="tpu_custom_call" | custom-call | tf_op jit(solution)/shard_map/pallas_call | solution.py:504
  144.6 19.1 %shard_map.86 = (f32[160,5760]{1,0:T(8,128)}, f32[160,4]{1,0:T(8,128)S(1)}) custom-call(s32[2]{0:T(128)S(1)} %pad_add_fusion.j_ref.at_ref, bf16[160,4096]{1,0:T(8,128)(2,1)S(1)} %copy-done.4, bf16[80,4096]{1,0:T(8,128)(2,1)} %collective-permute-done.12.xlt, bf16[80,4096]{1,0:T(8,128)(2,1)} %collective-permute-done.15.xlb, ...), custom_call_target="tpu_custom_call" | custom-call | tf_op jit(solution)/shard_map/pallas_call | solution.py:513
  (62 shorter events, 12.5 us)
Async XLA Ops:
  0.6 1.3 copy-start.2
  1.9 4.6 %copy-start.3 = (bf16[160,4096]{1,0:T(8,128)(2,1)S(1)}, bf16[160,4096]{1,0:T(8,128)(2,1)}, u32[]{:S(2)}) copy-start(bf16[160,4096]{1,0:T(8,128)(2,1)} %g_ref.5) | copy-start | bytes 3932164
  2.9 24.0 %collective-permute-start = (bf16[80,4096]{1,0:T(8,128)(2,1)S(1)}, bf16[80,4096]{1,0:T(8,128)(2,1)}, u32[]{:S(2)}, u32[]{:S(2)}) collective-permute-start(bf16[80,4096]{1,0:T(8,128)(2,1)S(1)} %get-tuple-element.56), channel_id=1, source_target_pairs={{0,1},{1,2},{2,3},{3,0},{4,5},{5,6},{6,7},{7,4},{8,9},{9,10},{10,1... | collective-permute-start | bytes 1966088 | tf_op jit(solution)/shard_map/ppermute | solution.py:406
  5.0 21.8 %collective-permute-start.1 = (bf16[80,4096]{1,0:T(8,128)(2,1)}, bf16[80,4096]{1,0:T(8,128)(2,1)}, u32[]{:S(2)}, u32[]{:S(2)}) collective-permute-start(bf16[80,4096]{1,0:T(8,128)(2,1)} %get-tuple-element.55), channel_id=1, source_target_pairs={{0,3},{1,0},{2,1},{3,2},{4,7},{5,4},{6,5},{7,6},{8,11},{9,8},{10,9... | collective-permute-start | bytes 1966088 | tf_op jit(solution)/shard_map/ppermute | solution.py:406
  6.5 2.0 %copy-start = (f32[1,160,5760]{2,1,0:T(8,128)S(1)}, f32[1,160,5760]{2,1,0:T(8,128)}, u32[]{:S(2)}) copy-start(f32[1,160,5760]{2,1,0:T(8,128)} %param.8) | copy-start | bytes 11059204
  9.2 6.0 %copy-start.7 = (bf16[160,5760]{1,0:T(8,128)(2,1)S(1)}, bf16[160,5760]{1,0:T(8,128)(2,1)}, u32[]{:S(2)}) copy-start(bf16[160,5760]{1,0:T(8,128)(2,1)} %k_ref) | copy-start | bytes 5529604
  11.4 15.4 %collective-permute-start.2 = (f32[8,3328]{1,0:T(8,128)S(1)}, f32[8,3328]{1,0:T(8,128)S(1)}, u32[]{:S(2)}, u32[]{:S(2)}) collective-permute-start(f32[8,3328]{1,0:T(8,128)S(1)} %get-tuple-element.48), channel_id=1, source_target_pairs={{0,1},{1,2},{2,3},{3,0},{4,5},{5,6},{6,7},{7,4},{8,9},{9,10},{10,1... | collective-permute-start | bytes 319496 | tf_op jit(solution)/shard_map/ppermute | solution.py:406
  11.5 15.3 %collective-permute-start.3 = (f32[8,3328]{1,0:T(8,128)S(1)}, f32[8,3328]{1,0:T(8,128)S(1)}, u32[]{:S(2)}, u32[]{:S(2)}) collective-permute-start(f32[8,3328]{1,0:T(8,128)S(1)} %get-tuple-element.49), channel_id=1, source_target_pairs={{0,2},{1,3},{2,0},{3,1},{4,6},{5,7},{6,4},{7,5},{8,10},{9,11},{10,... | collective-permute-start | bytes 319496 | tf_op jit(solution)/shard_map/ppermute | solution.py:406
  14.1 12.7 %collective-permute-start.4 = (f32[8,3328]{1,0:T(8,128)S(1)}, f32[8,3328]{1,0:T(8,128)S(1)}, u32[]{:S(2)}, u32[]{:S(2)}) collective-permute-start(f32[8,3328]{1,0:T(8,128)S(1)} %get-tuple-element.50), channel_id=1, source_target_pairs={{0,3},{1,0},{2,1},{3,2},{4,7},{5,4},{6,5},{7,6},{8,11},{9,8},{10,9... | collective-permute-start | bytes 319496 | tf_op jit(solution)/shard_map/ppermute | solution.py:406
  18.7 8.2 %copy-start.4 = (bf16[160,4096]{1,0:T(8,128)(2,1)S(1)}, bf16[160,4096]{1,0:T(8,128)(2,1)}, u32[]{:S(2)}) copy-start(bf16[160,4096]{1,0:T(8,128)(2,1)} %x0.1) | copy-start | bytes 3932164
  25.3 1.5 copy-start.5
  27.5 17.0 %collective-permute-start.5 = (bf16[80,4096]{1,0:T(8,128)(2,1)}, bf16[80,4096]{1,0:T(8,128)(2,1)S(1)}, u32[]{:S(2)}, u32[]{:S(2)}) collective-permute-start(bf16[80,4096]{1,0:T(8,128)(2,1)} %get-tuple-element.55), channel_id=1, source_target_pairs={{0,1},{1,2},{2,3},{3,0},{4,5},{5,6},{6,7},{7,4},{8,9},{9,10},{10,1... | collective-permute-start | bytes 1966088 | tf_op jit(solution)/shard_map/ppermute | solution.py:406
  28.0 17.3 %collective-permute-start.6 = (bf16[80,4096]{1,0:T(8,128)(2,1)S(1)}, bf16[80,4096]{1,0:T(8,128)(2,1)S(1)}, u32[]{:S(2)}, u32[]{:S(2)}) collective-permute-start(bf16[80,4096]{1,0:T(8,128)(2,1)S(1)} %get-tuple-element.56), channel_id=1, source_target_pairs={{0,3},{1,0},{2,1},{3,2},{4,7},{5,4},{6,5},{7,6},{8,11},{9,8},{10,9... | collective-permute-start | bytes 1966088 | tf_op jit(solution)/shard_map/ppermute | solution.py:406
  46.9 26.4 %collective-permute-start.10 = (bf16[80,4096]{1,0:T(8,128)(2,1)}, bf16[80,4096]{1,0:T(8,128)(2,1)}, u32[]{:S(2)}, u32[]{:S(2)}) collective-permute-start(bf16[80,4096]{1,0:T(8,128)(2,1)} %collective-permute-done.glt), channel_id=1, source_target_pairs={{0,1},{1,2},{2,3},{3,0},{4,5},{5,6},{6,7},{7,4},{8,9},{9,10},{10,1... | collective-permute-start | bytes 1966088 | tf_op jit(solution)/shard_map/ppermute | solution.py:406
  46.9 26.4 %collective-permute-start.11 = (bf16[80,4096]{1,0:T(8,128)(2,1)}, bf16[80,4096]{1,0:T(8,128)(2,1)}, u32[]{:S(2)}, u32[]{:S(2)}) collective-permute-start(bf16[80,4096]{1,0:T(8,128)(2,1)} %collective-permute-done.1.grb), channel_id=1, source_target_pairs={{0,3},{1,0},{2,1},{3,2},{4,7},{5,4},{6,5},{7,6},{8,11},{9,8},{10,9... | collective-permute-start | bytes 1966088 | tf_op jit(solution)/shard_map/ppermute | solution.py:406
  49.6 18.2 %all-to-all-start.1 = ((f32[8,8,1280]{2,1,0:T(8,128)}), f32[8,8,1280]{2,1,0:T(8,128)S(1)}, u32[]{:S(2)}, u32[]{:S(2)}) async-start(f32[8,8,1280]{2,1,0:T(8,128)} %shard_map.82), calls=%async_computation.1 | async-start | bytes 655360 | tf_op jit(solution)/shard_map/all_to_all | solution.py:425
  57.8 13.1 %collective-permute-start.7 = (bf16[256,512]{1,0:T(8,128)(2,1)}, bf16[256,512]{1,0:T(8,128)(2,1)S(1)}, u32[]{:S(2)}, u32[]{:S(2)}) collective-permute-start(bf16[256,512]{1,0:T(8,128)(2,1)} %copy-done.16), channel_id=1, source_target_pairs={{0,1},{1,2},{2,3},{3,0},{4,5},{5,6},{6,7},{7,4},{8,9},{9,10},{10,1... | collective-permute-start | bytes 786440 | tf_op jit(solution)/shard_map/ppermute | solution.py:406
  57.8 13.8 %collective-permute-start.8 = (bf16[256,512]{1,0:T(8,128)(2,1)}, bf16[256,512]{1,0:T(8,128)(2,1)}, u32[]{:S(2)}, u32[]{:S(2)}) collective-permute-start(bf16[256,512]{1,0:T(8,128)(2,1)} %copy-done.15), channel_id=1, source_target_pairs={{0,2},{1,3},{2,0},{3,1},{4,6},{5,7},{6,4},{7,5},{8,10},{9,11},{10,... | collective-permute-start | bytes 786440 | tf_op jit(solution)/shard_map/ppermute | solution.py:406
  59.0 14.4 %collective-permute-start.9 = (bf16[256,512]{1,0:T(8,128)(2,1)S(1)}, bf16[256,512]{1,0:T(8,128)(2,1)}, u32[]{:S(2)}, u32[]{:S(2)}) collective-permute-start(bf16[256,512]{1,0:T(8,128)(2,1)S(1)} %get-tuple-element.64), channel_id=1, source_target_pairs={{0,3},{1,0},{2,1},{3,2},{4,7},{5,4},{6,5},{7,6},{8,11},{9,8},{10,9... | collective-permute-start | bytes 786440 | tf_op jit(solution)/shard_map/ppermute | solution.py:406
  70.9 21.0 %copy-start.17 = (bf16[256,512]{1,0:T(8,128)(2,1)}, bf16[256,512]{1,0:T(8,128)(2,1)S(1)}, u32[]{:S(2)}) copy-start(bf16[256,512]{1,0:T(8,128)(2,1)S(1)} %collective-permute-done.7) | copy-start | bytes 786436
  84.1 37.4 %collective-permute-start.12 = (bf16[80,4096]{1,0:T(8,128)(2,1)}, bf16[80,4096]{1,0:T(8,128)(2,1)}, u32[]{:S(2)}, u32[]{:S(2)}) collective-permute-start(bf16[80,4096]{1,0:T(8,128)(2,1)} %get-tuple-element.68), channel_id=1, source_target_pairs={{0,1},{1,2},{2,3},{3,0},{4,5},{5,6},{6,7},{7,4},{8,9},{9,10},{10,1... | collective-permute-start | bytes 1966088 | tf_op jit(solution)/shard_map/ppermute | solution.py:406
  84.4 37.1 %collective-permute-start.13 = (bf16[80,4096]{1,0:T(8,128)(2,1)}, bf16[80,4096]{1,0:T(8,128)(2,1)}, u32[]{:S(2)}, u32[]{:S(2)}) collective-permute-start(bf16[80,4096]{1,0:T(8,128)(2,1)} %get-tuple-element.69), channel_id=1, source_target_pairs={{0,3},{1,0},{2,1},{3,2},{4,7},{5,4},{6,5},{7,6},{8,11},{9,8},{10,9... | collective-permute-start | bytes 1966088 | tf_op jit(solution)/shard_map/ppermute | solution.py:406
  86.8 2.0 %copy-start.1 = (f32[1,160,5760]{2,1,0:T(8,128)S(1)}, f32[1,160,5760]{2,1,0:T(8,128)}, u32[]{:S(2)}) copy-start(f32[1,160,5760]{2,1,0:T(8,128)} %param.8) | copy-start | bytes 11059204
  92.6 28.9 %all-to-all-start.3 = ((f32[64,8,128]{2,1,0:T(8,128)}), f32[64,8,128]{2,1,0:T(8,128)}, u32[]{:S(2)}, u32[]{:S(2)}) async-start(f32[64,8,128]{2,1,0:T(8,128)} %get-tuple-element.71), calls=%async_computation.3 | async-start | bytes 524288 | tf_op jit(solution)/shard_map/all_to_all | solution.py:500
  110.8 13.4 %collective-permute-start.14 = (bf16[3,256,512]{2,1,0:T(8,128)(2,1)S(1)}, bf16[3,256,512]{2,1,0:T(8,128)(2,1)}, u32[]{:S(2)}, u32[]{:S(2)}) collective-permute-start(bf16[3,256,512]{2,1,0:T(8,128)(2,1)S(1)} %pad_maximum_fusion.mine_ref), channel_id=1, source_target_pairs={{0,4},{4,0},{8,12},{12,8},{16,20},{20,16},{24,28},{28,24},{32,36},... | collective-permute-start | bytes 2359304 | tf_op jit(solution)/shard_map/ppermute | solution.py:487
  111.4 33.1 %collective-permute-start.15 = (bf16[80,4096]{1,0:T(8,128)(2,1)}, bf16[80,4096]{1,0:T(8,128)(2,1)}, u32[]{:S(2)}, u32[]{:S(2)}) collective-permute-start(bf16[80,4096]{1,0:T(8,128)(2,1)} %get-tuple-element.69), channel_id=1, source_target_pairs={{0,1},{1,2},{2,3},{3,0},{4,5},{5,6},{6,7},{7,4},{8,9},{9,10},{10,1... | collective-permute-start | bytes 1966088 | tf_op jit(solution)/shard_map/ppermute | solution.py:406
  111.4 33.1 %collective-permute-start.16 = (bf16[80,4096]{1,0:T(8,128)(2,1)}, bf16[80,4096]{1,0:T(8,128)(2,1)}, u32[]{:S(2)}, u32[]{:S(2)}) collective-permute-start(bf16[80,4096]{1,0:T(8,128)(2,1)} %get-tuple-element.68), channel_id=1, source_target_pairs={{0,3},{1,0},{2,1},{3,2},{4,7},{5,4},{6,5},{7,6},{8,11},{9,8},{10,9... | collective-permute-start | bytes 1966088 | tf_op jit(solution)/shard_map/ppermute | solution.py:406
  121.5 23.0 %collective-permute-start.17 = (bf16[80,4096]{1,0:T(8,128)(2,1)}, bf16[80,4096]{1,0:T(8,128)(2,1)S(1)}, u32[]{:S(2)}, u32[]{:S(2)}) collective-permute-start(bf16[80,4096]{1,0:T(8,128)(2,1)} %collective-permute-done.12.xlt), channel_id=1, source_target_pairs={{0,1},{1,2},{2,3},{3,0},{4,5},{5,6},{6,7},{7,4},{8,9},{9,10},{10,1... | collective-permute-start | bytes 1966088 | tf_op jit(solution)/shard_map/ppermute | solution.py:406
  121.5 23.0 %collective-permute-start.18 = (bf16[80,4096]{1,0:T(8,128)(2,1)}, bf16[80,4096]{1,0:T(8,128)(2,1)S(1)}, u32[]{:S(2)}, u32[]{:S(2)}) collective-permute-start(bf16[80,4096]{1,0:T(8,128)(2,1)} %collective-permute-done.13.xrb), channel_id=1, source_target_pairs={{0,3},{1,0},{2,1},{3,2},{4,7},{5,4},{6,5},{7,6},{8,11},{9,8},{10,9... | collective-permute-start | bytes 1966088 | tf_op jit(solution)/shard_map/ppermute | solution.py:406
  124.2 1.7 %copy-start.6 = (f32[160,4096]{1,0:T(8,128)S(1)}, f32[160,4096]{1,0:T(8,128)}, u32[]{:S(2)}) copy-start(f32[160,4096]{1,0:T(8,128)} %copy-done.5) | copy-start | bytes 7864324
  125.9 1.1 copy-start.9
  128.1 16.4 %copy-start.13 = (f32[64,640]{1,0:T(8,128)S(1)}, f32[64,640]{1,0:T(8,128)}, u32[]{:S(2)}) copy-start(f32[64,640]{1,0:T(8,128)} %copy-done.12) | copy-start | bytes 491524
  (7 other events, 5.5 us)

commit v2 on v1

--- a/solution.py
+++ b/solution.py
@@ -498,7 +498,7 @@
         16,
     )(theirs, err, g)
     q_got = lax.all_to_all(q_part, "dp", 0, 0, tiled=True)
-    xlt, xrb, q_got = lax.optimization_barrier((xlt, xrb, q_got))
+    xlt, xrb = after(xlt, q_part), after(xrb, q_part)
     xa, xo = around(xlt, 1), around(xrb, 3)
 
     in_grad = call(

time: 165 us -> 165 us (level)
  blocking collectives: 25 us -> 56 us
  starting transfers between devices: 49.3 us -> 34.5 us
  waiting for transfers between devices: 18.6 us -> 10.8 us
  local copies, waits for them, and re-layouts: 15.9 us -> 10.3 us
  Pallas kernels: 53.6 us -> 50.9 us
    all_to_all x0 -> x1, blocking collectives: none -> 31.3 us  [per_device(): q_got = lax.all_to_all(q_part, 'dp', 0, 0, tiled=True)]
    all_to_all x1 -> x0, starting transfers between devices: 17 us -> none  [per_device(): q_got = lax.all_to_all(q_part, 'dp', 0, 0, tiled=True)]
    all_to_all x1 -> x0, waiting for transfers between devices: 7.41 us -> none  [per_device(): q_got = lax.all_to_all(q_part, 'dp', 0, 0, tiled=True)]
    unnamed x37 -> x35, local copies, waits for them, and re-layouts: 15.9 us -> 10.3 us
    ppermute x1, starting transfers between devices: 0.62 us -> 5.16 us  [per_device(): k_other = lax.ppermute(k_mine, 'dp', [(i, i ^ 1) for i in range(workers)])]
    ppermute x18, starting transfers between devices: 23.5 us -> 21.2 us  [around(): return lax.ppermute(array, 'chan', [(i, (i + s) % 4) for i in range(4)])]
  transfers between devices with their start and end apart: 21 -> 20, of which waited for: 5 -> 5; matrix products, arithmetic and copies ran while one was open for 1% -> 1% of each run, Pallas kernels for 20% -> 18%
where the time goes in v2:
time: 165 us
  blocking collectives  56 us (34%)
  Pallas kernels  50.9 us (31%)
  starting transfers between devices  34.5 us (21%)
  waiting for transfers between devices  10.8 us (7%)
  local copies, waits for them, and re-layouts  10.3 us (6%)
    all_to_all x1, blocking collectives, per_device(): q_got = lax.all_to_all(q_part, 'dp', 0, 0, tiled=True)  31.3 us
    ppermute x18, starting transfers between devices, around(): return lax.ppermute(array, 'chan', [(i, (i + s) % 4) for i in range(4)])  21.2 us
    pallas_call x1, Pallas kernels, per_device(): call(weight_kernel, [sds((ch, TAPS * 640), F32), sds((ch, 4), F32)], [plt...  18.3 us
    pallas_call x1, Pallas kernels, per_device(): call(rest_kernel, sds((ch, CELLS), BF16), [pltpu.VMEM((3, SIDE, SIDE), BF...  16.2 us
    all_to_all x1, blocking collectives, exchanged(): lax.all_to_all(array, 'dp', 0, 0, axis_index_groups=line_groups(axis), ti...  14.2 us
    all_to_all x1, blocking collectives, per_device(): theirs = lax.all_to_all(mine, 'chan', 0, 0, tiled=True)  10.5 us
    unnamed x35, local copies, waits for them, and re-layouts  10.3 us
    all_to_all x1, starting transfers between devices, exchanged(): lax.all_to_all(array, 'dp', 0, 0, axis_index_groups=line_groups(axis), ti...  8.19 us
  transfers between devices with their start and end apart: 20, of which 5 were waited for; matrix products, arithmetic and copies ran while one was open for 1% of the time, Pallas kernels for 18%

profile of v2, /device:TPU:1, one launch (start us, length us, event | category | flops | bytes accessed | tf_op | source)
XLA Modules:
  0.0 164.6 jit_solution(269351927202352319)
XLA Ops:
  0.6 1.3 copy-done.2
  1.9 1.1 shard_map.77
  3.1 2.1 %collective-permute-start = (bf16[80,4096]{1,0:T(8,128)(2,1)}, bf16[80,4096]{1,0:T(8,128)(2,1)}, u32[]{:S(2)}, u32[]{:S(2)}) collective-permute-start(bf16[80,4096]{1,0:T(8,128)(2,1)} %get-tuple-element.55), channel_id=1, source_target_pairs={{0,1},{1,2},{2,3},{3,0},{4,5},{5,6},{6,7},{7,4},{8,9},{9,10},{10,1... | collective-permute-start | bytes 1966088 | tf_op jit(solution)/shard_map/ppermute | solution.py:406
  5.2 1.4 collective-permute-start.1
  6.7 2.0 %copy-done = f32[1,160,5760]{2,1,0:T(8,128)S(1)} copy-done((f32[1,160,5760]{2,1,0:T(8,128)S(1)}, f32[1,160,5760]{2,1,0:T(8,128)}, u32[]{:S(2)}) %copy-start) | copy-done | bytes 3686424
  9.5 2.2 %shard_map.78 = (f32[8,3328]{1,0:T(8,128)S(1)}, f32[8,3328]{1,0:T(8,128)S(1)}, f32[8,3328]{1,0:T(8,128)S(1)}, f32[8,3328]{1,0:T(8,128)S(1)}) custom-call(s32[2]{0:T(128)S(1)} %pad_add_fusion.j_ref.at_ref, f32[4,160]{1,0:T(4,128)S(1)} %bitcast.11, bf16[160,4096]{1,0:T(8,128)(2,1)S(1)} %copy-done.3, f32[160,5760]{1,0:T(8,128)S(1)} %bitcast.9), custom_call_target="tpu_custom_call" | custom-call | tf_op jit(solution)/shard_map/pallas_call | solution.py:441
  11.7 2.6 %collective-permute-start.3 = (f32[8,3328]{1,0:T(8,128)S(1)}, f32[8,3328]{1,0:T(8,128)S(1)}, u32[]{:S(2)}, u32[]{:S(2)}) collective-permute-start(f32[8,3328]{1,0:T(8,128)S(1)} %get-tuple-element.48), channel_id=1, source_target_pairs={{0,2},{1,3},{2,0},{3,1},{4,6},{5,7},{6,4},{7,5},{8,10},{9,11},{10,... | collective-permute-start | bytes 319496 | tf_op jit(solution)/shard_map/ppermute | solution.py:406
  14.3 1.1 collective-permute-start.4
  15.4 2.1 %shard_map.79 = (bf16[512,512]{1,0:T(8,128)(2,1)S(1)}, bf16[256,512]{1,0:T(8,128)(2,1)S(1)}, bf16[256,512]{1,0:T(8,128)(2,1)S(1)}, bf16[256,512]{1,0:T(8,128)(2,1)S(1)}) custom-call(s32[2]{0:T(128)S(1)} %pad_add_fusion.j_ref.at_ref, bf16[160,5760]{1,0:T(8,128)(2,1)S(1)} %copy-done.7), custom_call_target="tpu_custom_call" | custom-call | tf_op jit(solution)/shard_map/pallas_call | solution.py:456
  18.2 6.7 %shard_map.80.acc_ref = f32[160,4096]{1,0:T(8,128)S(1)} custom-call(bf16[512,512]{1,0:T(8,128)(2,1)S(1)} %get-tuple-element.51.k_ref, bf16[160,4096]{1,0:T(8,128)(2,1)S(1)} %copy-done.3), custom_call_target="tpu_custom_call" | custom-call | tf_op jit(solution)/shard_map/pallas_call | solution.py:464
  24.9 1.5 copy-done.5
  27.5 2.3 %collective-permute-start.6 = (bf16[80,4096]{1,0:T(8,128)(2,1)}, bf16[80,4096]{1,0:T(8,128)(2,1)S(1)}, u32[]{:S(2)}, u32[]{:S(2)}) collective-permute-start(bf16[80,4096]{1,0:T(8,128)(2,1)} %get-tuple-element.55), channel_id=1, source_target_pairs={{0,3},{1,0},{2,1},{3,2},{4,7},{5,4},{6,5},{7,6},{8,11},{9,8},{10,9... | collective-permute-start | bytes 1966088 | tf_op jit(solution)/shard_map/ppermute | solution.py:406
  29.9 14.2 %all_to_all.20.got = f32[8,8,1280]{2,1,0:T(8,128)S(1)} all-to-all(f32[8,8,1280]{2,1,0:T(8,128)S(1)} %shard_map.81), channel_id=1, replica_groups={{0,4,64,68,128,132,192,196},{8,12,72,76,136,140,200,204},{16,20,80,84,1..., dimensions={0} | all-to-all | bytes 655360 | tf_op jit(solution)/shard_map/all_to_all | solution.py:425
  46.5 2.7 %collective-permute-start.11 = (bf16[80,4096]{1,0:T(8,128)(2,1)}, bf16[80,4096]{1,0:T(8,128)(2,1)}, u32[]{:S(2)}, u32[]{:S(2)}) collective-permute-start(bf16[80,4096]{1,0:T(8,128)(2,1)} %collective-permute-done.1.grb), channel_id=1, source_target_pairs={{0,3},{1,0},{2,1},{3,2},{4,7},{5,4},{6,5},{7,6},{8,11},{9,8},{10,9... | collective-permute-start | bytes 1966088 | tf_op jit(solution)/shard_map/ppermute | solution.py:406
  49.1 8.2 %all-to-all-start.1 = ((f32[8,8,1280]{2,1,0:T(8,128)}), f32[8,8,1280]{2,1,0:T(8,128)S(1)}, u32[]{:S(2)}, u32[]{:S(2)}) async-start(f32[8,8,1280]{2,1,0:T(8,128)} %shard_map.82), calls=%async_computation.1 | async-start | bytes 655360 | tf_op jit(solution)/shard_map/all_to_all | solution.py:425
  57.3 1.2 collective-permute-start.8
  58.5 1.5 collective-permute-start.9
  60.1 0.8 copy-done.13
  61.8 5.6 %all-to-all-done.1.s_ref = f32[8,8,1280]{2,1,0:T(8,128)S(1)} async-done(((f32[8,8,1280]{2,1,0:T(8,128)}), f32[8,8,1280]{2,1,0:T(8,128)S(1)}, u32[]{:S(2)}, u32[]{:S(2)}) %all-to-all-start.1) | async-done | bytes 327712 | tf_op jit(solution)/shard_map/all_to_all | solution.py:425
  68.0 2.5 %collective-permute-done.7 = bf16[256,512]{1,0:T(8,128)(2,1)} collective-permute-done((bf16[256,512]{1,0:T(8,128)(2,1)}, bf16[256,512]{1,0:T(8,128)(2,1)}, u32[]{:S(2)}, u32[]{:S(2)}) %collective-permute-start.7) | collective-permute-done | bytes 262176 | tf_op jit(solution)/shard_map/ppermute | solution.py:406
  71.2 1.9 %collective-permute-done.9 = bf16[256,512]{1,0:T(8,128)(2,1)} collective-permute-done((bf16[256,512]{1,0:T(8,128)(2,1)S(1)}, bf16[256,512]{1,0:T(8,128)(2,1)}, u32[]{:S(2)}, u32[]{:S(2)}) %collective-permute-start.9) | collective-permute-done | bytes 262176 | tf_op jit(solution)/shard_map/ppermute | solution.py:406
  73.1 10.5 %all_to_all.21.blocks = f32[4,8,3328]{2,1,0:T(8,128)S(1)} all-to-all(f32[4,8,3328]{2,1,0:T(8,128)S(1)} %shard_map.83), channel_id=1, replica_groups=mesh['dp'=64,'chan'=4] {'chan'}, dimensions={0} | all-to-all | bytes 851968 | tf_op jit(solution)/shard_map/all_to_all | solution.py:488
  83.6 0.9 collective-permute-start.16
  85.1 1.2 pad_maximum_fusion.mine_ref
  86.3 5.2 %collective-permute-start.12 = (bf16[3,256,512]{2,1,0:T(8,128)(2,1)S(1)}, bf16[3,256,512]{2,1,0:T(8,128)(2,1)S(1)}, u32[]{:S(2)}, u32[]{:S(2)}) collective-permute-start(bf16[3,256,512]{2,1,0:T(8,128)(2,1)S(1)} %pad_maximum_fusion.mine_ref), channel_id=1, source_target_pairs={{0,4},{4,0},{8,12},{12,8},{16,20},{20,16},{24,28},{28,24},{32,36},... | collective-permute-start | bytes 2359304 | tf_op jit(solution)/shard_map/ppermute | solution.py:487
  91.5 1.2 collective-permute-start.14
  92.7 1.5 collective-permute-start.15
  94.2 2.4 %shard_map.84 = (f32[64,640]{1,0:T(8,128)S(1)}, f32[64,8,128]{2,1,0:T(8,128)S(1)}) custom-call(f32[4,8,3328]{2,1,0:T(8,128)S(1)} %all_to_all.21.blocks, f32[160,5760]{1,0:T(8,128)S(1)} %bitcast.10, bf16[160,4096]{1,0:T(8,128)(2,1)S(1)} %copy-done.3), custom_call_target="tpu_custom_call" | custom-call | tf_op jit(solution)/shard_map/pallas_call | solution.py:492
  96.5 1.3 collective-permute-start.18
  98.1 31.3 %all_to_all.22.got = f32[64,8,128]{2,1,0:T(8,128)S(1)} all-to-all(f32[64,8,128]{2,1,0:T(8,128)S(1)} %get-tuple-element.68), channel_id=1, replica_groups=mesh['dp'=64,'chan'=4] {'dp'}, dimensions={0} | all-to-all | bytes 524288 | tf_op jit(solution)/shard_map/all_to_all | solution.py:500
  129.4 16.2 %shard_map.85 = bf16[160,4096]{1,0:T(8,128)(2,1)} custom-call(s32[2]{0:T(128)S(1)} %pad_add_fusion.j_ref.at_ref, bf16[3,256,512]{2,1,0:T(8,128)(2,1)S(1)} %pad_maximum_fusion.mine_ref, bf16[3,256,512]{2,1,0:T(8,128)(2,1)S(1)} %collective-permute-done.12.other_ref, bf16[80,4096]{1,0:T(8,128)(2,1)} %collective-permute-done.glt, ...), custom_call_target="tpu_custom_call" | custom-call | tf_op jit(solution)/shard_map/pallas_call | solution.py:504
  145.6 18.3 %shard_map.86 = (f32[160,5760]{1,0:T(8,128)}, f32[160,4]{1,0:T(8,128)S(1)}) custom-call(s32[2]{0:T(128)S(1)} %pad_add_fusion.j_ref.at_ref, bf16[160,4096]{1,0:T(8,128)(2,1)S(1)} %copy-done.4, bf16[80,4096]{1,0:T(8,128)(2,1)S(1)} %collective-permute-done.13.xlt, bf16[80,4096]{1,0:T(8,128)(2,1)S(1)} %collective-permute-done.14.xlb, ...), custom_call_target="tpu_custom_call" | custom-call | tf_op jit(solution)/shard_map/pallas_call | solution.py:513
  (59 shorter events, 8.9 us)
Async XLA Ops:
  0.6 1.3 copy-start.2
  1.9 4.8 %copy-start.3 = (bf16[160,4096]{1,0:T(8,128)(2,1)S(1)}, bf16[160,4096]{1,0:T(8,128)(2,1)}, u32[]{:S(2)}) copy-start(bf16[160,4096]{1,0:T(8,128)(2,1)} %g_ref.5) | copy-start | bytes 3932164
  3.1 23.3 %collective-permute-start = (bf16[80,4096]{1,0:T(8,128)(2,1)}, bf16[80,4096]{1,0:T(8,128)(2,1)}, u32[]{:S(2)}, u32[]{:S(2)}) collective-permute-start(bf16[80,4096]{1,0:T(8,128)(2,1)} %get-tuple-element.55), channel_id=1, source_target_pairs={{0,1},{1,2},{2,3},{3,0},{4,5},{5,6},{6,7},{7,4},{8,9},{9,10},{10,1... | collective-permute-start | bytes 1966088 | tf_op jit(solution)/shard_map/ppermute | solution.py:406
  5.2 21.2 %collective-permute-start.1 = (bf16[80,4096]{1,0:T(8,128)(2,1)}, bf16[80,4096]{1,0:T(8,128)(2,1)}, u32[]{:S(2)}, u32[]{:S(2)}) collective-permute-start(bf16[80,4096]{1,0:T(8,128)(2,1)} %get-tuple-element.54), channel_id=1, source_target_pairs={{0,3},{1,0},{2,1},{3,2},{4,7},{5,4},{6,5},{7,6},{8,11},{9,8},{10,9... | collective-permute-start | bytes 1966088 | tf_op jit(solution)/shard_map/ppermute | solution.py:406
  6.7 2.0 %copy-start = (f32[1,160,5760]{2,1,0:T(8,128)S(1)}, f32[1,160,5760]{2,1,0:T(8,128)}, u32[]{:S(2)}) copy-start(f32[1,160,5760]{2,1,0:T(8,128)} %param.8) | copy-start | bytes 11059204
  9.5 6.0 %copy-start.7 = (bf16[160,5760]{1,0:T(8,128)(2,1)S(1)}, bf16[160,5760]{1,0:T(8,128)(2,1)}, u32[]{:S(2)}) copy-start(bf16[160,5760]{1,0:T(8,128)(2,1)} %k_ref) | copy-start | bytes 5529604
  11.6 14.7 %collective-permute-start.2 = (f32[8,3328]{1,0:T(8,128)S(1)}, f32[8,3328]{1,0:T(8,128)S(1)}, u32[]{:S(2)}, u32[]{:S(2)}) collective-permute-start(f32[8,3328]{1,0:T(8,128)S(1)} %get-tuple-element.47), channel_id=1, source_target_pairs={{0,1},{1,2},{2,3},{3,0},{4,5},{5,6},{6,7},{7,4},{8,9},{9,10},{10,1... | collective-permute-start | bytes 319496 | tf_op jit(solution)/shard_map/ppermute | solution.py:406
  11.7 14.7 %collective-permute-start.3 = (f32[8,3328]{1,0:T(8,128)S(1)}, f32[8,3328]{1,0:T(8,128)S(1)}, u32[]{:S(2)}, u32[]{:S(2)}) collective-permute-start(f32[8,3328]{1,0:T(8,128)S(1)} %get-tuple-element.48), channel_id=1, source_target_pairs={{0,2},{1,3},{2,0},{3,1},{4,6},{5,7},{6,4},{7,5},{8,10},{9,11},{10,... | collective-permute-start | bytes 319496 | tf_op jit(solution)/shard_map/ppermute | solution.py:406
  14.3 12.1 %collective-permute-start.4 = (f32[8,3328]{1,0:T(8,128)S(1)}, f32[8,3328]{1,0:T(8,128)S(1)}, u32[]{:S(2)}, u32[]{:S(2)}) collective-permute-start(f32[8,3328]{1,0:T(8,128)S(1)} %get-tuple-element.49), channel_id=1, source_target_pairs={{0,3},{1,0},{2,1},{3,2},{4,7},{5,4},{6,5},{7,6},{8,11},{9,8},{10,9... | collective-permute-start | bytes 319496 | tf_op jit(solution)/shard_map/ppermute | solution.py:406
  18.2 8.3 %copy-start.4 = (bf16[160,4096]{1,0:T(8,128)(2,1)S(1)}, bf16[160,4096]{1,0:T(8,128)(2,1)}, u32[]{:S(2)}) copy-start(bf16[160,4096]{1,0:T(8,128)(2,1)} %x0.1) | copy-start | bytes 3932164
  24.9 1.5 copy-start.5
  27.1 16.9 %collective-permute-start.5 = (bf16[80,4096]{1,0:T(8,128)(2,1)}, bf16[80,4096]{1,0:T(8,128)(2,1)S(1)}, u32[]{:S(2)}, u32[]{:S(2)}) collective-permute-start(bf16[80,4096]{1,0:T(8,128)(2,1)} %get-tuple-element.54), channel_id=1, source_target_pairs={{0,1},{1,2},{2,3},{3,0},{4,5},{5,6},{6,7},{7,4},{8,9},{9,10},{10,1... | collective-permute-start | bytes 1966088 | tf_op jit(solution)/shard_map/ppermute | solution.py:406
  27.5 17.3 %collective-permute-start.6 = (bf16[80,4096]{1,0:T(8,128)(2,1)}, bf16[80,4096]{1,0:T(8,128)(2,1)S(1)}, u32[]{:S(2)}, u32[]{:S(2)}) collective-permute-start(bf16[80,4096]{1,0:T(8,128)(2,1)} %get-tuple-element.55), channel_id=1, source_target_pairs={{0,3},{1,0},{2,1},{3,2},{4,7},{5,4},{6,5},{7,6},{8,11},{9,8},{10,9... | collective-permute-start | bytes 1966088 | tf_op jit(solution)/shard_map/ppermute | solution.py:406
  46.5 26.6 %collective-permute-start.10 = (bf16[80,4096]{1,0:T(8,128)(2,1)}, bf16[80,4096]{1,0:T(8,128)(2,1)}, u32[]{:S(2)}, u32[]{:S(2)}) collective-permute-start(bf16[80,4096]{1,0:T(8,128)(2,1)} %collective-permute-done.glt), channel_id=1, source_target_pairs={{0,1},{1,2},{2,3},{3,0},{4,5},{5,6},{6,7},{7,4},{8,9},{9,10},{10,1... | collective-permute-start | bytes 1966088 | tf_op jit(solution)/shard_map/ppermute | solution.py:406
  46.5 26.6 %collective-permute-start.11 = (bf16[80,4096]{1,0:T(8,128)(2,1)}, bf16[80,4096]{1,0:T(8,128)(2,1)}, u32[]{:S(2)}, u32[]{:S(2)}) collective-permute-start(bf16[80,4096]{1,0:T(8,128)(2,1)} %collective-permute-done.1.grb), channel_id=1, source_target_pairs={{0,3},{1,0},{2,1},{3,2},{4,7},{5,4},{6,5},{7,6},{8,11},{9,8},{10,9... | collective-permute-start | bytes 1966088 | tf_op jit(solution)/shard_map/ppermute | solution.py:406
  49.1 18.2 %all-to-all-start.1 = ((f32[8,8,1280]{2,1,0:T(8,128)}), f32[8,8,1280]{2,1,0:T(8,128)S(1)}, u32[]{:S(2)}, u32[]{:S(2)}) async-start(f32[8,8,1280]{2,1,0:T(8,128)} %shard_map.82), calls=%async_computation.1 | async-start | bytes 655360 | tf_op jit(solution)/shard_map/all_to_all | solution.py:425
  57.3 13.1 %collective-permute-start.7 = (bf16[256,512]{1,0:T(8,128)(2,1)}, bf16[256,512]{1,0:T(8,128)(2,1)}, u32[]{:S(2)}, u32[]{:S(2)}) collective-permute-start(bf16[256,512]{1,0:T(8,128)(2,1)} %copy-done.16), channel_id=1, source_target_pairs={{0,1},{1,2},{2,3},{3,0},{4,5},{5,6},{6,7},{7,4},{8,9},{9,10},{10,1... | collective-permute-start | bytes 786440 | tf_op jit(solution)/shard_map/ppermute | solution.py:406
  57.3 13.8 %collective-permute-start.8 = (bf16[256,512]{1,0:T(8,128)(2,1)S(1)}, bf16[256,512]{1,0:T(8,128)(2,1)}, u32[]{:S(2)}, u32[]{:S(2)}) collective-permute-start(bf16[256,512]{1,0:T(8,128)(2,1)S(1)} %get-tuple-element.62), channel_id=1, source_target_pairs={{0,2},{1,3},{2,0},{3,1},{4,6},{5,7},{6,4},{7,5},{8,10},{9,11},{10,... | collective-permute-start | bytes 786440 | tf_op jit(solution)/shard_map/ppermute | solution.py:406
  58.5 14.5 %collective-permute-start.9 = (bf16[256,512]{1,0:T(8,128)(2,1)S(1)}, bf16[256,512]{1,0:T(8,128)(2,1)}, u32[]{:S(2)}, u32[]{:S(2)}) collective-permute-start(bf16[256,512]{1,0:T(8,128)(2,1)S(1)} %get-tuple-element.63), channel_id=1, source_target_pairs={{0,3},{1,0},{2,1},{3,2},{4,7},{5,4},{6,5},{7,6},{8,11},{9,8},{10,9... | collective-permute-start | bytes 786440 | tf_op jit(solution)/shard_map/ppermute | solution.py:406
  60.1 0.9 copy-start.13
  67.4 25.3 %copy-start.14 = (bf16[80,4096]{1,0:T(8,128)(2,1)S(1)}, bf16[80,4096]{1,0:T(8,128)(2,1)}, u32[]{:S(2)}) copy-start(bf16[80,4096]{1,0:T(8,128)(2,1)} %copy-done.13) | copy-start | bytes 1966084
  67.4 26.8 %copy-start.1 = (f32[1,160,5760]{2,1,0:T(8,128)S(1)}, f32[1,160,5760]{2,1,0:T(8,128)}, u32[]{:S(2)}) copy-start(f32[1,160,5760]{2,1,0:T(8,128)} %param.8) | copy-start | bytes 11059204
  83.6 12.9 %collective-permute-start.16 = (bf16[80,4096]{1,0:T(8,128)(2,1)}, bf16[80,4096]{1,0:T(8,128)(2,1)S(1)}, u32[]{:S(2)}, u32[]{:S(2)}) collective-permute-start(bf16[80,4096]{1,0:T(8,128)(2,1)} %copy-done.15), channel_id=1, source_target_pairs={{0,3},{1,0},{2,1},{3,2},{4,7},{5,4},{6,5},{7,6},{8,11},{9,8},{10,9... | collective-permute-start | bytes 1966088 | tf_op jit(solution)/shard_map/ppermute | solution.py:406
  84.5 13.3 %collective-permute-start.13 = (bf16[80,4096]{1,0:T(8,128)(2,1)}, bf16[80,4096]{1,0:T(8,128)(2,1)S(1)}, u32[]{:S(2)}, u32[]{:S(2)}) collective-permute-start(bf16[80,4096]{1,0:T(8,128)(2,1)} %copy-done.13), channel_id=1, source_target_pairs={{0,1},{1,2},{2,3},{3,0},{4,5},{5,6},{6,7},{7,4},{8,9},{9,10},{10,1... | collective-permute-start | bytes 1966088 | tf_op jit(solution)/shard_map/ppermute | solution.py:406
  86.3 43.2 %copy-start.6 = (f32[160,4096]{1,0:T(8,128)S(1)}, f32[160,4096]{1,0:T(8,128)}, u32[]{:S(2)}) copy-start(f32[160,4096]{1,0:T(8,128)} %copy-done.5) | copy-start | bytes 7864324
  86.3 43.1 %copy-start.9 = (bf16[80,4096]{1,0:T(8,128)(2,1)S(1)}, bf16[80,4096]{1,0:T(8,128)(2,1)}, u32[]{:S(2)}) copy-start(bf16[80,4096]{1,0:T(8,128)(2,1)} %copy-done.8) | copy-start | bytes 1966084
  86.3 43.1 %copy-start.11 = (bf16[80,4096]{1,0:T(8,128)(2,1)S(1)}, bf16[80,4096]{1,0:T(8,128)(2,1)}, u32[]{:S(2)}) copy-start(bf16[80,4096]{1,0:T(8,128)(2,1)} %copy-done.10) | copy-start | bytes 1966084
  86.3 43.1 %collective-permute-start.12 = (bf16[3,256,512]{2,1,0:T(8,128)(2,1)S(1)}, bf16[3,256,512]{2,1,0:T(8,128)(2,1)S(1)}, u32[]{:S(2)}, u32[]{:S(2)}) collective-permute-start(bf16[3,256,512]{2,1,0:T(8,128)(2,1)S(1)} %pad_maximum_fusion.mine_ref), channel_id=1, source_target_pairs={{0,4},{4,0},{8,12},{12,8},{16,20},{20,16},{24,28},{28,24},{32,36},... | collective-permute-start | bytes 2359304 | tf_op jit(solution)/shard_map/ppermute | solution.py:487
  91.5 54.1 %collective-permute-start.14 = (bf16[80,4096]{1,0:T(8,128)(2,1)}, bf16[80,4096]{1,0:T(8,128)(2,1)S(1)}, u32[]{:S(2)}, u32[]{:S(2)}) collective-permute-start(bf16[80,4096]{1,0:T(8,128)(2,1)} %copy-done.15), channel_id=1, source_target_pairs={{0,1},{1,2},{2,3},{3,0},{4,5},{5,6},{6,7},{7,4},{8,9},{9,10},{10,1... | collective-permute-start | bytes 1966088 | tf_op jit(solution)/shard_map/ppermute | solution.py:406
  92.7 52.9 %collective-permute-start.15 = (bf16[80,4096]{1,0:T(8,128)(2,1)S(1)}, bf16[80,4096]{1,0:T(8,128)(2,1)S(1)}, u32[]{:S(2)}, u32[]{:S(2)}) collective-permute-start(bf16[80,4096]{1,0:T(8,128)(2,1)S(1)} %copy-done.14), channel_id=1, source_target_pairs={{0,3},{1,0},{2,1},{3,2},{4,7},{5,4},{6,5},{7,6},{8,11},{9,8},{10,9... | collective-permute-start | bytes 1966088 | tf_op jit(solution)/shard_map/ppermute | solution.py:406
  96.5 49.1 %collective-permute-start.18 = (bf16[80,4096]{1,0:T(8,128)(2,1)S(1)}, bf16[80,4096]{1,0:T(8,128)(2,1)S(1)}, u32[]{:S(2)}, u32[]{:S(2)}) collective-permute-start(bf16[80,4096]{1,0:T(8,128)(2,1)S(1)} %collective-permute-done.16.xrb), channel_id=1, source_target_pairs={{0,3},{1,0},{2,1},{3,2},{4,7},{5,4},{6,5},{7,6},{8,11},{9,8},{10,9... | collective-permute-start | bytes 1966088 | tf_op jit(solution)/shard_map/ppermute | solution.py:406
  97.8 47.8 %collective-permute-start.17 = (bf16[80,4096]{1,0:T(8,128)(2,1)S(1)}, bf16[80,4096]{1,0:T(8,128)(2,1)S(1)}, u32[]{:S(2)}, u32[]{:S(2)}) collective-permute-start(bf16[80,4096]{1,0:T(8,128)(2,1)S(1)} %collective-permute-done.13.xlt), channel_id=1, source_target_pairs={{0,1},{1,2},{2,3},{3,0},{4,5},{5,6},{6,7},{7,4},{8,9},{9,10},{10,1... | collective-permute-start | bytes 1966088 | tf_op jit(solution)/shard_map/ppermute | solution.py:406
  (5 other events, 3.9 us)

commit v3 on v2

--- a/solution.py
+++ b/solution.py
@@ -508,7 +508,10 @@
         1,
         9,
         44,
-    )(after(at, q_got), k_mine, k_other, glt, glb, grt, grb, ga, go, acc)
+        cost_estimate=pl.CostEstimate(
+            flops=2 * 3 * ch * 3 * SIDE * CELLS, transcendentals=0, bytes_accessed=12 * ch * CELLS + 12 * SIDE * SIDE
+        ),
+    )(after(at, q_part), k_mine, k_other, glt, glb, grt, grb, ga, go, acc)
 
     new_error, q_factor = call(
         weight_kernel,

time: 165 us -> 163 us (0.988)
  blocking collectives: 56 us -> 14.2 us
  starting transfers between devices: 34.5 us -> 58.3 us
  local copies, waits for them, and re-layouts: 10.3 us -> 20.7 us
  waiting for transfers between devices: 10.8 us -> 13.4 us
  Pallas kernels: 50.9 us -> 52.9 us
    all_to_all x2 -> x0, blocking collectives: 41.9 us -> none  [the longest x1 31.3 us: per_device(): q_got = lax.all_to_all(q_part, 'dp', 0, 0, tiled=True)]
    all_to_all x0 -> x2, starting transfers between devices: none -> 23.5 us  [the longest x1 19 us: per_device(): q_got = lax.all_to_all(q_part, 'dp', 0, 0, tiled=True)]
    unnamed x35 -> x45, local copies, waits for them, and re-layouts: 10.3 us -> 20.7 us
    ppermute x18, starting transfers between devices: 21.2 us -> 23.4 us  [around(): return lax.ppermute(array, 'chan', [(i, (i + s) % 4) for i in range(4)])]
    ppermute x1, starting transfers between devices: 5.16 us -> 3.15 us  [per_device(): k_other = lax.ppermute(k_mine, 'dp', [(i, i ^ 1) for i in range(workers)])]
  transfers between devices with their start and end apart: 20 -> 22, of which waited for: 5 -> 6; matrix products, arithmetic and copies ran while one was open for 1% -> 1% of each run, Pallas kernels for 18% -> 19%
where the time goes in v3:
time: 163 us
  starting transfers between devices  58.3 us (36%)
  Pallas kernels  52.9 us (32%)
  local copies, waits for them, and re-layouts  20.7 us (13%)
  blocking collectives  14.2 us (9%)
  waiting for transfers between devices  13.4 us (8%)
  other arithmetic  2.17 us (1%)
    ppermute x18, starting transfers between devices, around(): return lax.ppermute(array, 'chan', [(i, (i + s) % 4) for i in range(4)])  23.4 us
    unnamed x45, local copies, waits for them, and re-layouts  20.7 us
    pallas_call x1, Pallas kernels, per_device(): call(weight_kernel, [sds((ch, TAPS * 640), F32), sds((ch, 4), F32)], [plt...  19.3 us
    all_to_all x1, starting transfers between devices, per_device(): q_got = lax.all_to_all(q_part, 'dp', 0, 0, tiled=True)  19 us
    pallas_call x1, Pallas kernels, per_device(): call(rest_kernel, sds((ch, CELLS), BF16), [pltpu.VMEM((3, SIDE, SIDE), BF...  16.6 us
    all_to_all x1, blocking collectives, exchanged(): lax.all_to_all(array, 'dp', 0, 0, axis_index_groups=line_groups(axis), ti...  14.2 us
    all_to_all x1, starting transfers between devices, exchanged(): lax.all_to_all(array, 'dp', 0, 0, axis_index_groups=line_groups(axis), ti...  8.19 us
    ppermute x18, waiting for transfers between devices, around(): return lax.ppermute(array, 'chan', [(i, (i + s) % 4) for i in range(4)])  6.71 us
  transfers between devices with their start and end apart: 22, of which 6 were waited for; matrix products, arithmetic and copies ran while one was open for 1% of the time, Pallas kernels for 19%

profile of v3, /device:TPU:1, one launch (start us, length us, event | category | flops | bytes accessed | tf_op | source)
XLA Modules:
  0.0 162.5 jit_solution(3707088496007222648)
XLA Ops:
  0.6 1.3 copy-done.2
  2.9 2.1 %collective-permute-start = (bf16[80,4096]{1,0:T(8,128)(2,1)S(1)}, bf16[80,4096]{1,0:T(8,128)(2,1)}, u32[]{:S(2)}, u32[]{:S(2)}) collective-permute-start(bf16[80,4096]{1,0:T(8,128)(2,1)S(1)} %get-tuple-element.55), channel_id=1, source_target_pairs={{0,1},{1,2},{2,3},{3,0},{4,5},{5,6},{6,7},{7,4},{8,9},{9,10},{10,1... | collective-permute-start | bytes 1966088 | tf_op jit(solution)/shard_map/ppermute | solution.py:406
  5.0 1.4 collective-permute-start.1
  6.5 2.0 %copy-done = f32[1,160,5760]{2,1,0:T(8,128)S(1)} copy-done((f32[1,160,5760]{2,1,0:T(8,128)S(1)}, f32[1,160,5760]{2,1,0:T(8,128)}, u32[]{:S(2)}) %copy-start) | copy-done | bytes 3686424
  9.2 2.2 %shard_map.78 = (f32[8,3328]{1,0:T(8,128)S(1)}, f32[8,3328]{1,0:T(8,128)S(1)}, f32[8,3328]{1,0:T(8,128)S(1)}, f32[8,3328]{1,0:T(8,128)S(1)}) custom-call(s32[2]{0:T(128)S(1)} %pad_add_fusion.j_ref.at_ref, f32[4,160]{1,0:T(4,128)S(1)} %bitcast.11, bf16[160,4096]{1,0:T(8,128)(2,1)S(1)} %copy-done.3, f32[160,5760]{1,0:T(8,128)S(1)} %bitcast.9), custom_call_target="tpu_custom_call" | custom-call | tf_op jit(solution)/shard_map/pallas_call | solution.py:441
  11.5 2.6 %collective-permute-start.3 = (f32[8,3328]{1,0:T(8,128)S(1)}, f32[8,3328]{1,0:T(8,128)S(1)}, u32[]{:S(2)}, u32[]{:S(2)}) collective-permute-start(f32[8,3328]{1,0:T(8,128)S(1)} %get-tuple-element.48), channel_id=1, source_target_pairs={{0,2},{1,3},{2,0},{3,1},{4,6},{5,7},{6,4},{7,5},{8,10},{9,11},{10,... | collective-permute-start | bytes 319496 | tf_op jit(solution)/shard_map/ppermute | solution.py:406
  15.2 2.1 %shard_map.79 = (bf16[512,512]{1,0:T(8,128)(2,1)S(1)}, bf16[256,512]{1,0:T(8,128)(2,1)S(1)}, bf16[256,512]{1,0:T(8,128)(2,1)S(1)}, bf16[256,512]{1,0:T(8,128)(2,1)S(1)}) custom-call(s32[2]{0:T(128)S(1)} %pad_add_fusion.j_ref.at_ref, bf16[160,5760]{1,0:T(8,128)(2,1)S(1)} %copy-done.7), custom_call_target="tpu_custom_call" | custom-call | tf_op jit(solution)/shard_map/pallas_call | solution.py:456
  18.7 6.7 %shard_map.80.acc_ref = f32[160,4096]{1,0:T(8,128)S(1)} custom-call(bf16[512,512]{1,0:T(8,128)(2,1)S(1)} %get-tuple-element.51.k_ref, bf16[160,4096]{1,0:T(8,128)(2,1)S(1)} %copy-done.3), custom_call_target="tpu_custom_call" | custom-call | tf_op jit(solution)/shard_map/pallas_call | solution.py:464
  25.4 1.5 copy-done.5
  28.0 2.3 %collective-permute-start.6 = (bf16[80,4096]{1,0:T(8,128)(2,1)S(1)}, bf16[80,4096]{1,0:T(8,128)(2,1)S(1)}, u32[]{:S(2)}, u32[]{:S(2)}) collective-permute-start(bf16[80,4096]{1,0:T(8,128)(2,1)S(1)} %get-tuple-element.55), channel_id=1, source_target_pairs={{0,3},{1,0},{2,1},{3,2},{4,7},{5,4},{6,5},{7,6},{8,11},{9,8},{10,9... | collective-permute-start | bytes 1966088 | tf_op jit(solution)/shard_map/ppermute | solution.py:406
  30.3 14.2 %all_to_all.20.got = f32[8,8,1280]{2,1,0:T(8,128)S(1)} all-to-all(f32[8,8,1280]{2,1,0:T(8,128)S(1)} %shard_map.81), channel_id=1, replica_groups={{0,4,64,68,128,132,192,196},{8,12,72,76,136,140,200,204},{16,20,80,84,1..., dimensions={0} | all-to-all | bytes 655360 | tf_op jit(solution)/shard_map/all_to_all | solution.py:425
  47.0 2.7 %collective-permute-start.11 = (bf16[80,4096]{1,0:T(8,128)(2,1)}, bf16[80,4096]{1,0:T(8,128)(2,1)}, u32[]{:S(2)}, u32[]{:S(2)}) collective-permute-start(bf16[80,4096]{1,0:T(8,128)(2,1)} %collective-permute-done.1.grb), channel_id=1, source_target_pairs={{0,3},{1,0},{2,1},{3,2},{4,7},{5,4},{6,5},{7,6},{8,11},{9,8},{10,9... | collective-permute-start | bytes 1966088 | tf_op jit(solution)/shard_map/ppermute | solution.py:406
  49.7 8.2 %all-to-all-start.1 = ((f32[8,8,1280]{2,1,0:T(8,128)}), f32[8,8,1280]{2,1,0:T(8,128)S(1)}, u32[]{:S(2)}, u32[]{:S(2)}) async-start(f32[8,8,1280]{2,1,0:T(8,128)} %shard_map.82), calls=%async_computation.1 | async-start | bytes 655360 | tf_op jit(solution)/shard_map/all_to_all | solution.py:425
  59.0 1.5 collective-permute-start.9
  62.3 5.6 %all-to-all-done.1.s_ref = f32[8,8,1280]{2,1,0:T(8,128)S(1)} async-done(((f32[8,8,1280]{2,1,0:T(8,128)}), f32[8,8,1280]{2,1,0:T(8,128)S(1)}, u32[]{:S(2)}, u32[]{:S(2)}) %all-to-all-start.1) | async-done | bytes 327712 | tf_op jit(solution)/shard_map/all_to_all | solution.py:425
  67.9 1.3 shard_map.83
  69.2 1.8 %collective-permute-done.7 = bf16[256,512]{1,0:T(8,128)(2,1)S(1)} collective-permute-done((bf16[256,512]{1,0:T(8,128)(2,1)}, bf16[256,512]{1,0:T(8,128)(2,1)S(1)}, u32[]{:S(2)}, u32[]{:S(2)}) %collective-permute-start.7) | collective-permute-done | bytes 262176 | tf_op jit(solution)/shard_map/ppermute | solution.py:406
  71.7 1.7 %collective-permute-done.9 = bf16[256,512]{1,0:T(8,128)(2,1)} collective-permute-done((bf16[256,512]{1,0:T(8,128)(2,1)S(1)}, bf16[256,512]{1,0:T(8,128)(2,1)}, u32[]{:S(2)}, u32[]{:S(2)}) %collective-permute-start.9) | collective-permute-done | bytes 262176 | tf_op jit(solution)/shard_map/ppermute | solution.py:406
  73.4 4.6 %all-to-all-start.2 = ((f32[4,8,3328]{2,1,0:T(8,128)}), f32[4,8,3328]{2,1,0:T(8,128)S(1)}, u32[]{:S(2)}, u32[]{:S(2)}) async-start(f32[4,8,3328]{2,1,0:T(8,128)} %shard_map.83), calls=%async_computation.2 | async-start | bytes 851968 | tf_op jit(solution)/shard_map/all_to_all | solution.py:488
  78.0 2.1 %pad_maximum_fusion.mine_ref = bf16[3,256,512]{2,1,0:T(8,128)(2,1)} fusion(bf16[1,256,512]{2,1,0:T(8,128)(2,1)} %bitcast.6, bf16[1,256,512]{2,1,0:T(8,128)(2,1)} %bitcast.5, bf16[1,256,512]{2,1,0:T(8,128)(2,1)} %bitcast.12), kind=kLoop, calls=%fused_computation | loop fusion | flops 786432 | bytes 1572864 | tf_op jit(solution)/shard_map/stack | solution.py:486
  80.1 3.2 %collective-permute-start.12 = (bf16[3,256,512]{2,1,0:T(8,128)(2,1)}, bf16[3,256,512]{2,1,0:T(8,128)(2,1)}, u32[]{:S(2)}, u32[]{:S(2)}) collective-permute-start(bf16[3,256,512]{2,1,0:T(8,128)(2,1)} %pad_maximum_fusion.mine_ref), channel_id=1, source_target_pairs={{0,4},{4,0},{8,12},{12,8},{16,20},{20,16},{24,28},{28,24},{32,36},... | collective-permute-start | bytes 2359304 | tf_op jit(solution)/shard_map/ppermute | solution.py:487
  84.4 1.8 %collective-permute-start.16 = (bf16[80,4096]{1,0:T(8,128)(2,1)}, bf16[80,4096]{1,0:T(8,128)(2,1)}, u32[]{:S(2)}, u32[]{:S(2)}) collective-permute-start(bf16[80,4096]{1,0:T(8,128)(2,1)} %copy-done.18), channel_id=1, source_target_pairs={{0,3},{1,0},{2,1},{3,2},{4,7},{5,4},{6,5},{7,6},{8,11},{9,8},{10,9... | collective-permute-start | bytes 1966088 | tf_op jit(solution)/shard_map/ppermute | solution.py:406
  86.4 2.5 %collective-permute-start.15 = (bf16[80,4096]{1,0:T(8,128)(2,1)}, bf16[80,4096]{1,0:T(8,128)(2,1)}, u32[]{:S(2)}, u32[]{:S(2)}) collective-permute-start(bf16[80,4096]{1,0:T(8,128)(2,1)} %copy-done.17), channel_id=1, source_target_pairs={{0,3},{1,0},{2,1},{3,2},{4,7},{5,4},{6,5},{7,6},{8,11},{9,8},{10,9... | collective-permute-start | bytes 1966088 | tf_op jit(solution)/shard_map/ppermute | solution.py:406
  88.9 2.0 %copy-done.1 = f32[1,160,5760]{2,1,0:T(8,128)S(1)} copy-done((f32[1,160,5760]{2,1,0:T(8,128)S(1)}, f32[1,160,5760]{2,1,0:T(8,128)}, u32[]{:S(2)}) %copy-start.1) | copy-done | bytes 3686424
  90.9 2.4 %shard_map.84 = (f32[64,640]{1,0:T(8,128)S(1)}, f32[64,8,128]{2,1,0:T(8,128)S(1)}) custom-call(f32[4,8,3328]{2,1,0:T(8,128)S(1)} %all-to-all-done.2.blocks, f32[160,5760]{1,0:T(8,128)S(1)} %bitcast.10, bf16[160,4096]{1,0:T(8,128)(2,1)S(1)} %copy-done.3), custom_call_target="tpu_custom_call" | custom-call | tf_op jit(solution)/shard_map/pallas_call | solution.py:492
  94.7 2.5 %collective-permute-done.16.xrb = bf16[80,4096]{1,0:T(8,128)(2,1)} collective-permute-done((bf16[80,4096]{1,0:T(8,128)(2,1)}, bf16[80,4096]{1,0:T(8,128)(2,1)}, u32[]{:S(2)}, u32[]{:S(2)}) %collective-permute-start.16) | collective-permute-done | bytes 655392 | tf_op jit(solution)/shard_map/ppermute | solution.py:406
  97.1 3.4 %collective-permute-start.18 = (bf16[80,4096]{1,0:T(8,128)(2,1)}, bf16[80,4096]{1,0:T(8,128)(2,1)S(1)}, u32[]{:S(2)}, u32[]{:S(2)}) collective-permute-start(bf16[80,4096]{1,0:T(8,128)(2,1)} %collective-permute-done.16.xrb), channel_id=1, source_target_pairs={{0,3},{1,0},{2,1},{3,2},{4,7},{5,4},{6,5},{7,6},{8,11},{9,8},{10,9... | collective-permute-start | bytes 1966088 | tf_op jit(solution)/shard_map/ppermute | solution.py:406
  100.6 19.0 %all-to-all-start.3 = ((f32[64,8,128]{2,1,0:T(8,128)}), f32[64,8,128]{2,1,0:T(8,128)S(1)}, u32[]{:S(2)}, u32[]{:S(2)}) async-start(f32[64,8,128]{2,1,0:T(8,128)} %copy-done.8), calls=%async_computation.3 | async-start | bytes 524288 | tf_op jit(solution)/shard_map/all_to_all | solution.py:500
  119.6 1.7 %copy-done.6 = f32[160,4096]{1,0:T(8,128)S(1)} copy-done((f32[160,4096]{1,0:T(8,128)S(1)}, f32[160,4096]{1,0:T(8,128)}, u32[]{:S(2)}) %copy-start.6) | copy-done | bytes 2621464
  123.5 16.6 %shard_map.85 = bf16[160,4096]{1,0:T(8,128)(2,1)} custom-call(s32[2]{0:T(128)S(1)} %pad_add_fusion.j_ref.at_ref, bf16[3,256,512]{2,1,0:T(8,128)(2,1)} %pad_maximum_fusion.mine_ref, bf16[3,256,512]{2,1,0:T(8,128)(2,1)} %collective-permute-done.12.other_ref, bf16[80,4096]{1,0:T(8,128)(2,1)} %collective-permute-done.glt, bf16[80,4096]{1,0:T(8,128)(2,1)S(1)} %copy-done.14, ...), custom_call_target="tpu_custom_call" | custom-call | flops 6039797760 | bytes 11010048 | tf_op jit(solution)/shard_map/pallas_call | solution.py:504
  141.0 19.3 %shard_map.86 = (f32[160,5760]{1,0:T(8,128)}, f32[160,4]{1,0:T(8,128)S(1)}) custom-call(s32[2]{0:T(128)S(1)} %pad_add_fusion.j_ref.at_ref, bf16[160,4096]{1,0:T(8,128)(2,1)S(1)} %copy-done.4, bf16[80,4096]{1,0:T(8,128)(2,1)} %collective-permute-done.13.xlt, bf16[80,4096]{1,0:T(8,128)(2,1)} %collective-permute-done.14.xlb, ...), custom_call_target="tpu_custom_call" | custom-call | tf_op jit(solution)/shard_map/pallas_call | solution.py:516
  161.0 1.6 copy.8
  (71 shorter events, 18.0 us)
Async XLA Ops:
  0.6 1.3 copy-start.2
  1.9 4.6 %copy-start.3 = (bf16[160,4096]{1,0:T(8,128)(2,1)S(1)}, bf16[160,4096]{1,0:T(8,128)(2,1)}, u32[]{:S(2)}) copy-start(bf16[160,4096]{1,0:T(8,128)(2,1)} %g_ref.5) | copy-start | bytes 3932164
  2.9 24.0 %collective-permute-start = (bf16[80,4096]{1,0:T(8,128)(2,1)S(1)}, bf16[80,4096]{1,0:T(8,128)(2,1)}, u32[]{:S(2)}, u32[]{:S(2)}) collective-permute-start(bf16[80,4096]{1,0:T(8,128)(2,1)S(1)} %get-tuple-element.55), channel_id=1, source_target_pairs={{0,1},{1,2},{2,3},{3,0},{4,5},{5,6},{6,7},{7,4},{8,9},{9,10},{10,1... | collective-permute-start | bytes 1966088 | tf_op jit(solution)/shard_map/ppermute | solution.py:406
  5.0 21.9 %collective-permute-start.1 = (bf16[80,4096]{1,0:T(8,128)(2,1)}, bf16[80,4096]{1,0:T(8,128)(2,1)}, u32[]{:S(2)}, u32[]{:S(2)}) collective-permute-start(bf16[80,4096]{1,0:T(8,128)(2,1)} %get-tuple-element.54), channel_id=1, source_target_pairs={{0,3},{1,0},{2,1},{3,2},{4,7},{5,4},{6,5},{7,6},{8,11},{9,8},{10,9... | collective-permute-start | bytes 1966088 | tf_op jit(solution)/shard_map/ppermute | solution.py:406
  6.5 2.0 %copy-start = (f32[1,160,5760]{2,1,0:T(8,128)S(1)}, f32[1,160,5760]{2,1,0:T(8,128)}, u32[]{:S(2)}) copy-start(f32[1,160,5760]{2,1,0:T(8,128)} %param.8) | copy-start | bytes 11059204
  9.2 6.0 %copy-start.7 = (bf16[160,5760]{1,0:T(8,128)(2,1)S(1)}, bf16[160,5760]{1,0:T(8,128)(2,1)}, u32[]{:S(2)}) copy-start(bf16[160,5760]{1,0:T(8,128)(2,1)} %k_ref) | copy-start | bytes 5529604
  11.4 15.5 %collective-permute-start.2 = (f32[8,3328]{1,0:T(8,128)S(1)}, f32[8,3328]{1,0:T(8,128)S(1)}, u32[]{:S(2)}, u32[]{:S(2)}) collective-permute-start(f32[8,3328]{1,0:T(8,128)S(1)} %get-tuple-element.47), channel_id=1, source_target_pairs={{0,1},{1,2},{2,3},{3,0},{4,5},{5,6},{6,7},{7,4},{8,9},{9,10},{10,1... | collective-permute-start | bytes 319496 | tf_op jit(solution)/shard_map/ppermute | solution.py:406
  11.5 15.4 %collective-permute-start.3 = (f32[8,3328]{1,0:T(8,128)S(1)}, f32[8,3328]{1,0:T(8,128)S(1)}, u32[]{:S(2)}, u32[]{:S(2)}) collective-permute-start(f32[8,3328]{1,0:T(8,128)S(1)} %get-tuple-element.48), channel_id=1, source_target_pairs={{0,2},{1,3},{2,0},{3,1},{4,6},{5,7},{6,4},{7,5},{8,10},{9,11},{10,... | collective-permute-start | bytes 319496 | tf_op jit(solution)/shard_map/ppermute | solution.py:406
  14.1 12.8 %collective-permute-start.4 = (f32[8,3328]{1,0:T(8,128)S(1)}, f32[8,3328]{1,0:T(8,128)S(1)}, u32[]{:S(2)}, u32[]{:S(2)}) collective-permute-start(f32[8,3328]{1,0:T(8,128)S(1)} %get-tuple-element.49), channel_id=1, source_target_pairs={{0,3},{1,0},{2,1},{3,2},{4,7},{5,4},{6,5},{7,6},{8,11},{9,8},{10,9... | collective-permute-start | bytes 319496 | tf_op jit(solution)/shard_map/ppermute | solution.py:406
  18.7 8.2 %copy-start.4 = (bf16[160,4096]{1,0:T(8,128)(2,1)S(1)}, bf16[160,4096]{1,0:T(8,128)(2,1)}, u32[]{:S(2)}) copy-start(bf16[160,4096]{1,0:T(8,128)(2,1)} %x0.1) | copy-start | bytes 3932164
  25.4 1.5 copy-start.5
  27.6 17.0 %collective-permute-start.5 = (bf16[80,4096]{1,0:T(8,128)(2,1)}, bf16[80,4096]{1,0:T(8,128)(2,1)S(1)}, u32[]{:S(2)}, u32[]{:S(2)}) collective-permute-start(bf16[80,4096]{1,0:T(8,128)(2,1)} %get-tuple-element.54), channel_id=1, source_target_pairs={{0,1},{1,2},{2,3},{3,0},{4,5},{5,6},{6,7},{7,4},{8,9},{9,10},{10,1... | collective-permute-start | bytes 1966088 | tf_op jit(solution)/shard_map/ppermute | solution.py:406
  28.0 17.3 %collective-permute-start.6 = (bf16[80,4096]{1,0:T(8,128)(2,1)S(1)}, bf16[80,4096]{1,0:T(8,128)(2,1)S(1)}, u32[]{:S(2)}, u32[]{:S(2)}) collective-permute-start(bf16[80,4096]{1,0:T(8,128)(2,1)S(1)} %get-tuple-element.55), channel_id=1, source_target_pairs={{0,3},{1,0},{2,1},{3,2},{4,7},{5,4},{6,5},{7,6},{8,11},{9,8},{10,9... | collective-permute-start | bytes 1966088 | tf_op jit(solution)/shard_map/ppermute | solution.py:406
  47.0 26.4 %collective-permute-start.10 = (bf16[80,4096]{1,0:T(8,128)(2,1)}, bf16[80,4096]{1,0:T(8,128)(2,1)}, u32[]{:S(2)}, u32[]{:S(2)}) collective-permute-start(bf16[80,4096]{1,0:T(8,128)(2,1)} %collective-permute-done.glt), channel_id=1, source_target_pairs={{0,1},{1,2},{2,3},{3,0},{4,5},{5,6},{6,7},{7,4},{8,9},{9,10},{10,1... | collective-permute-start | bytes 1966088 | tf_op jit(solution)/shard_map/ppermute | solution.py:406
  47.0 26.4 %collective-permute-start.11 = (bf16[80,4096]{1,0:T(8,128)(2,1)}, bf16[80,4096]{1,0:T(8,128)(2,1)}, u32[]{:S(2)}, u32[]{:S(2)}) collective-permute-start(bf16[80,4096]{1,0:T(8,128)(2,1)} %collective-permute-done.1.grb), channel_id=1, source_target_pairs={{0,3},{1,0},{2,1},{3,2},{4,7},{5,4},{6,5},{7,6},{8,11},{9,8},{10,9... | collective-permute-start | bytes 1966088 | tf_op jit(solution)/shard_map/ppermute | solution.py:406
  49.7 18.2 %all-to-all-start.1 = ((f32[8,8,1280]{2,1,0:T(8,128)}), f32[8,8,1280]{2,1,0:T(8,128)S(1)}, u32[]{:S(2)}, u32[]{:S(2)}) async-start(f32[8,8,1280]{2,1,0:T(8,128)} %shard_map.82), calls=%async_computation.1 | async-start | bytes 655360 | tf_op jit(solution)/shard_map/all_to_all | solution.py:425
  57.8 13.1 %collective-permute-start.7 = (bf16[256,512]{1,0:T(8,128)(2,1)}, bf16[256,512]{1,0:T(8,128)(2,1)S(1)}, u32[]{:S(2)}, u32[]{:S(2)}) collective-permute-start(bf16[256,512]{1,0:T(8,128)(2,1)} %copy-done.20), channel_id=1, source_target_pairs={{0,1},{1,2},{2,3},{3,0},{4,5},{5,6},{6,7},{7,4},{8,9},{9,10},{10,1... | collective-permute-start | bytes 786440 | tf_op jit(solution)/shard_map/ppermute | solution.py:406
  57.8 13.8 %collective-permute-start.8 = (bf16[256,512]{1,0:T(8,128)(2,1)}, bf16[256,512]{1,0:T(8,128)(2,1)}, u32[]{:S(2)}, u32[]{:S(2)}) collective-permute-start(bf16[256,512]{1,0:T(8,128)(2,1)} %copy-done.19), channel_id=1, source_target_pairs={{0,2},{1,3},{2,0},{3,1},{4,6},{5,7},{6,4},{7,5},{8,10},{9,11},{10,... | collective-permute-start | bytes 786440 | tf_op jit(solution)/shard_map/ppermute | solution.py:406
  59.0 14.4 %collective-permute-start.9 = (bf16[256,512]{1,0:T(8,128)(2,1)S(1)}, bf16[256,512]{1,0:T(8,128)(2,1)}, u32[]{:S(2)}, u32[]{:S(2)}) collective-permute-start(bf16[256,512]{1,0:T(8,128)(2,1)S(1)} %get-tuple-element.63), channel_id=1, source_target_pairs={{0,3},{1,0},{2,1},{3,2},{4,7},{5,4},{6,5},{7,6},{8,11},{9,8},{10,9... | collective-permute-start | bytes 786440 | tf_op jit(solution)/shard_map/ppermute | solution.py:406
  71.0 2.4 %copy-start.21 = (bf16[256,512]{1,0:T(8,128)(2,1)}, bf16[256,512]{1,0:T(8,128)(2,1)S(1)}, u32[]{:S(2)}) copy-start(bf16[256,512]{1,0:T(8,128)(2,1)S(1)} %collective-permute-done.7) | copy-start | bytes 786436
  73.4 11.0 %all-to-all-start.2 = ((f32[4,8,3328]{2,1,0:T(8,128)}), f32[4,8,3328]{2,1,0:T(8,128)S(1)}, u32[]{:S(2)}, u32[]{:S(2)}) async-start(f32[4,8,3328]{2,1,0:T(8,128)} %shard_map.83), calls=%async_computation.2 | async-start | bytes 851968 | tf_op jit(solution)/shard_map/all_to_all | solution.py:488
  80.1 39.5 %collective-permute-start.12 = (bf16[3,256,512]{2,1,0:T(8,128)(2,1)}, bf16[3,256,512]{2,1,0:T(8,128)(2,1)}, u32[]{:S(2)}, u32[]{:S(2)}) collective-permute-start(bf16[3,256,512]{2,1,0:T(8,128)(2,1)} %pad_maximum_fusion.mine_ref), channel_id=1, source_target_pairs={{0,4},{4,0},{8,12},{12,8},{16,20},{20,16},{24,28},{28,24},{32,36},... | collective-permute-start | bytes 2359304 | tf_op jit(solution)/shard_map/ppermute | solution.py:487
  84.4 12.7 %collective-permute-start.16 = (bf16[80,4096]{1,0:T(8,128)(2,1)}, bf16[80,4096]{1,0:T(8,128)(2,1)}, u32[]{:S(2)}, u32[]{:S(2)}) collective-permute-start(bf16[80,4096]{1,0:T(8,128)(2,1)} %copy-done.18), channel_id=1, source_target_pairs={{0,3},{1,0},{2,1},{3,2},{4,7},{5,4},{6,5},{7,6},{8,11},{9,8},{10,9... | collective-permute-start | bytes 1966088 | tf_op jit(solution)/shard_map/ppermute | solution.py:406
  86.2 14.4 %collective-permute-start.13 = (bf16[80,4096]{1,0:T(8,128)(2,1)}, bf16[80,4096]{1,0:T(8,128)(2,1)}, u32[]{:S(2)}, u32[]{:S(2)}) collective-permute-start(bf16[80,4096]{1,0:T(8,128)(2,1)} %copy-done.17), channel_id=1, source_target_pairs={{0,1},{1,2},{2,3},{3,0},{4,5},{5,6},{6,7},{7,4},{8,9},{9,10},{10,1... | collective-permute-start | bytes 1966088 | tf_op jit(solution)/shard_map/ppermute | solution.py:406
  86.2 53.9 %collective-permute-start.14 = (bf16[80,4096]{1,0:T(8,128)(2,1)}, bf16[80,4096]{1,0:T(8,128)(2,1)}, u32[]{:S(2)}, u32[]{:S(2)}) collective-permute-start(bf16[80,4096]{1,0:T(8,128)(2,1)} %copy-done.18), channel_id=1, source_target_pairs={{0,1},{1,2},{2,3},{3,0},{4,5},{5,6},{6,7},{7,4},{8,9},{9,10},{10,1... | collective-permute-start | bytes 1966088 | tf_op jit(solution)/shard_map/ppermute | solution.py:406
  86.4 53.6 %collective-permute-start.15 = (bf16[80,4096]{1,0:T(8,128)(2,1)}, bf16[80,4096]{1,0:T(8,128)(2,1)}, u32[]{:S(2)}, u32[]{:S(2)}) collective-permute-start(bf16[80,4096]{1,0:T(8,128)(2,1)} %copy-done.17), channel_id=1, source_target_pairs={{0,3},{1,0},{2,1},{3,2},{4,7},{5,4},{6,5},{7,6},{8,11},{9,8},{10,9... | collective-permute-start | bytes 1966088 | tf_op jit(solution)/shard_map/ppermute | solution.py:406
  88.9 2.0 %copy-start.1 = (f32[1,160,5760]{2,1,0:T(8,128)S(1)}, f32[1,160,5760]{2,1,0:T(8,128)}, u32[]{:S(2)}) copy-start(f32[1,160,5760]{2,1,0:T(8,128)} %param.8) | copy-start | bytes 11059204
  97.1 43.0 %collective-permute-start.18 = (bf16[80,4096]{1,0:T(8,128)(2,1)}, bf16[80,4096]{1,0:T(8,128)(2,1)S(1)}, u32[]{:S(2)}, u32[]{:S(2)}) collective-permute-start(bf16[80,4096]{1,0:T(8,128)(2,1)} %collective-permute-done.16.xrb), channel_id=1, source_target_pairs={{0,3},{1,0},{2,1},{3,2},{4,7},{5,4},{6,5},{7,6},{8,11},{9,8},{10,9... | collective-permute-start | bytes 1966088 | tf_op jit(solution)/shard_map/ppermute | solution.py:406
  100.5 39.6 %collective-permute-start.17 = (bf16[80,4096]{1,0:T(8,128)(2,1)}, bf16[80,4096]{1,0:T(8,128)(2,1)}, u32[]{:S(2)}, u32[]{:S(2)}) collective-permute-start(bf16[80,4096]{1,0:T(8,128)(2,1)} %collective-permute-done.13.xlt), channel_id=1, source_target_pairs={{0,1},{1,2},{2,3},{3,0},{4,5},{5,6},{6,7},{7,4},{8,9},{9,10},{10,1... | collective-permute-start | bytes 1966088 | tf_op jit(solution)/shard_map/ppermute | solution.py:406
  100.6 39.5 %all-to-all-start.3 = ((f32[64,8,128]{2,1,0:T(8,128)}), f32[64,8,128]{2,1,0:T(8,128)S(1)}, u32[]{:S(2)}, u32[]{:S(2)}) async-start(f32[64,8,128]{2,1,0:T(8,128)} %copy-done.8), calls=%async_computation.3 | async-start | bytes 524288 | tf_op jit(solution)/shard_map/all_to_all | solution.py:500
  119.5 1.7 %copy-start.6 = (f32[160,4096]{1,0:T(8,128)S(1)}, f32[160,4096]{1,0:T(8,128)}, u32[]{:S(2)}) copy-start(f32[160,4096]{1,0:T(8,128)} %copy-done.5) | copy-start | bytes 7864324
  121.3 1.1 copy-start.14
  (12 other events, 9.5 us)
